TPU v7x, 256 devices: a whole 4x4x8 slice. The times are simulated.
256 devices in a mesh: section: 16 (over y, x), ctx: 16 (over z, core).
Axes of the slice: x: 4, y: 4, z: 8, core: 2. Of those that a mesh axis runs over, the one named last changes fastest.
Arguments:
- query_fwd: bfloat16 [16, 2048, 4096], P('section', 'ctx'), may hold values from -100 to 100
- key_fwd: bfloat16 [16, 2048, 512], P('section', 'ctx'), may hold values from -4.5 to 4.5
- value_fwd: bfloat16 [16, 2048, 512], P('section', 'ctx'), may hold values from -6 to 6
- doc_len_fwd: int32 [16, 16], P('section'), may hold values from 1 to 384, 2048 in all within a row
- query_bwd: bfloat16 [16, 2048, 4096], P('section', 'ctx'), may hold values from -100 to 100
- key_bwd: bfloat16 [16, 2048, 512], P('section', 'ctx'), may hold values from -4.5 to 4.5
- value_bwd: bfloat16 [16, 2048, 512], P('section', 'ctx'), may hold values from -6 to 6
- doc_len_bwd: int32 [16, 16], P('section'), may hold values from 1 to 384, 2048 in all within a row
- grad_held: bfloat16 [16, 2048, 4096], P('section', 'ctx'), may hold values from -6 to 6
Outputs:
- next_stream: bfloat16 [16, 2048, 4096], P('section', 'ctx')
- grad_query: bfloat16 [16, 2048, 4096], P('section', 'ctx')
- grad_key: bfloat16 [16, 2048, 512], P('section', 'ctx')
- grad_value: bfloat16 [16, 2048, 512], P('section', 'ctx')
Inputs may be any that keep to these rules, and one draw needn't show every extreme that they name: `doc_len_fwd`: each row holds the 16 document lengths of one packed micro-batch in order, summing to 2048; the longest is exactly 384. `doc_len_bwd`: each row holds the 16 document lengths of one packed micro-batch in order, summing to 2048; the longest is exactly 384.
All inputs are finite; a program needn't handle non-finite values.
Results may differ from a plain program's by a relative error of at most 0.007.
Values may be sent and summed in bfloat16 or wider, within the bound.
No kernel may reach another device: no remote copies, remote signals or barrier semaphores. Data moves between devices by JAX's collectives and lax.ppermute only.
A program may use at most 64 MiB of HBM per device.

v0:
```python
import jax
import jax.numpy as jnp
from jax import lax
from jax.sharding import PartitionSpec as P

HEADS = 32
KV_HEADS = 4
HEAD_DIM = 128
REACH = 3


MASKED_SCORE = -1e30


def from_behind(value, axis, steps):
    count = lax.axis_size(axis)
    first, last = (max(0, -steps), min(count, count - steps))
    return lax.ppermute(value, axis, [(source, source + steps) for source in range(first, last)])


def doc_index(lengths, positions):
    doc_ends = jnp.cumsum(lengths)
    return jnp.sum((positions[:, None] >= doc_ends[None, :]).astype(jnp.int32), axis=1)


def piece_mask(lengths, query_doc, query_pos, first_row, piece_rows):
    key_pos = first_row + jnp.arange(piece_rows, dtype=jnp.int32)
    key_doc = doc_index(lengths, key_pos)
    same_doc = query_doc[:, None] == key_doc[None, :]
    causal = key_pos[None, :] <= query_pos[:, None]
    return same_doc & causal & (key_pos[None, :] >= 0)


def fold_piece(running, piece_kv, allowed, queries, score_scale):
    max_run, total_run, accum = running
    piece_rows = piece_kv.shape[0]
    kv_width = KV_HEADS * HEAD_DIM
    key_rows = piece_kv[:, :kv_width].reshape(piece_rows, KV_HEADS, HEAD_DIM)
    value_rows = piece_kv[:, kv_width:].reshape(piece_rows, KV_HEADS, HEAD_DIM)
    new_max, new_total, new_accum = ([], [], [])
    for kv_group in range(KV_HEADS):
        scores = (
            jnp.einsum(
                "qhd,kd->hqk",
                queries[:, kv_group],
                key_rows[:, kv_group],
                preferred_element_type=jnp.float32,
            )
            * score_scale
        )
        scores = jnp.where(allowed[None], scores, MASKED_SCORE)
        row_max = jnp.maximum(max_run[kv_group], jnp.max(scores, axis=-1))
        rescale = jnp.exp(max_run[kv_group] - row_max)
        weights = jnp.where(allowed[None], jnp.exp(scores - row_max[..., None]), 0.0)
        value_sum = jnp.einsum(
            "hqk,kd->qhd",
            weights.astype(jnp.bfloat16),
            value_rows[:, kv_group],
            preferred_element_type=jnp.float32,
        )
        new_max.append(row_max)
        new_total.append(total_run[kv_group] * rescale + jnp.sum(weights, axis=-1))
        new_accum.append(accum[:, kv_group] * rescale.T[:, :, None] + value_sum)
    return (jnp.stack(new_max), jnp.stack(new_total), jnp.stack(new_accum, axis=1))


def stat_piece(stats, piece_kv, allowed, queries, out_grad, score_scale):
    max_run, total_run, delta_run = stats
    piece_rows = piece_kv.shape[0]
    kv_width = KV_HEADS * HEAD_DIM
    key_rows = piece_kv[:, :kv_width].reshape(piece_rows, KV_HEADS, HEAD_DIM)
    value_rows = piece_kv[:, kv_width:].reshape(piece_rows, KV_HEADS, HEAD_DIM)
    new_max, new_total, new_delta = ([], [], [])
    for kv_group in range(KV_HEADS):
        scores = (
            jnp.einsum(
                "qhd,kd->hqk",
                queries[:, kv_group],
                key_rows[:, kv_group],
                preferred_element_type=jnp.float32,
            )
            * score_scale
        )
        scores = jnp.where(allowed[None], scores, MASKED_SCORE)
        row_max = jnp.maximum(max_run[kv_group], jnp.max(scores, axis=-1))
        rescale = jnp.exp(max_run[kv_group] - row_max)
        weights = jnp.where(allowed[None], jnp.exp(scores - row_max[..., None]), 0.0)
        d_prob = jnp.einsum(
            "qhd,kd->hqk",
            out_grad[:, kv_group],
            value_rows[:, kv_group],
            preferred_element_type=jnp.float32,
        )
        new_max.append(row_max)
        new_total.append(total_run[kv_group] * rescale + jnp.sum(weights, axis=-1))
        new_delta.append(delta_run[kv_group] * rescale + jnp.sum(weights * d_prob, axis=-1))
    return (jnp.stack(new_max), jnp.stack(new_total), jnp.stack(new_delta))


def grad_piece(piece_kv, allowed, queries, out_grad, max_all, total_all, delta_all, score_scale):
    piece_rows = piece_kv.shape[0]
    kv_width = KV_HEADS * HEAD_DIM
    key_rows = piece_kv[:, :kv_width].reshape(piece_rows, KV_HEADS, HEAD_DIM)
    value_rows = piece_kv[:, kv_width:].reshape(piece_rows, KV_HEADS, HEAD_DIM)
    query_terms, key_terms, value_terms = ([], [], [])
    for kv_group in range(KV_HEADS):
        scores = (
            jnp.einsum(
                "qhd,kd->hqk",
                queries[:, kv_group],
                key_rows[:, kv_group],
                preferred_element_type=jnp.float32,
            )
            * score_scale
        )
        scores = jnp.where(allowed[None], scores, MASKED_SCORE)
        weights = jnp.where(allowed[None], jnp.exp(scores - max_all[kv_group][..., None]), 0.0)
        probabilities = weights / total_all[kv_group][..., None]
        d_prob = jnp.einsum(
            "qhd,kd->hqk",
            out_grad[:, kv_group],
            value_rows[:, kv_group],
            preferred_element_type=jnp.float32,
        )
        d_score = (probabilities * (d_prob - delta_all[kv_group][..., None])).astype(jnp.bfloat16)
        low_probs = probabilities.astype(jnp.bfloat16)
        query_terms.append(
            jnp.einsum(
                "hqk,kd->qhd", d_score, key_rows[:, kv_group], preferred_element_type=jnp.float32
            )
            * score_scale
        )
        key_terms.append(
            jnp.einsum(
                "hqk,qhd->kd", d_score, queries[:, kv_group], preferred_element_type=jnp.float32
            )
            * score_scale
        )
        value_terms.append(
            jnp.einsum(
                "hqk,qhd->kd", low_probs, out_grad[:, kv_group], preferred_element_type=jnp.float32
            )
        )
    key_part = jnp.stack(key_terms, axis=1).reshape(piece_rows, kv_width)
    value_part = jnp.stack(value_terms, axis=1).reshape(piece_rows, kv_width)
    part = jnp.concatenate([key_part, value_part], axis=1).astype(jnp.bfloat16).astype(jnp.float32)
    return (jnp.stack(query_terms, axis=1), part)


def on_device(
    query_fwd,
    key_fwd,
    value_fwd,
    doc_len_fwd,
    query_bwd,
    key_bwd,
    value_bwd,
    doc_len_bwd,
    grad_held,
):
    row_count = query_fwd.shape[1]
    shard_spot = lax.axis_index("ctx")
    query_pos = shard_spot * row_count + jnp.arange(row_count, dtype=jnp.int32)
    score_scale = HEAD_DIM ** (-0.5)
    group_size = HEADS // KV_HEADS
    kv_width = KV_HEADS * HEAD_DIM
    lengths_fwd = doc_len_fwd[0]
    query_doc_fwd = doc_index(lengths_fwd, query_pos)
    queries_fwd = query_fwd[0].reshape(row_count, KV_HEADS, group_size, HEAD_DIM)
    packed_fwd = jnp.concatenate([key_fwd[0], value_fwd[0]], axis=1)
    initial = (
        jnp.full((KV_HEADS, group_size, row_count), MASKED_SCORE, jnp.float32),
        jnp.zeros((KV_HEADS, group_size, row_count), jnp.float32),
        jnp.zeros((row_count, KV_HEADS, group_size, HEAD_DIM), jnp.float32),
    )

    def absorb(running, piece_kv, first_row):
        allowed = piece_mask(lengths_fwd, query_doc_fwd, query_pos, first_row, piece_kv.shape[0])
        return fold_piece(running, piece_kv, allowed, queries_fwd, score_scale)

    running = absorb(initial, packed_fwd, shard_spot * row_count)

    def advance_fixed(step_index, carry):
        current, moved = carry
        moved = from_behind(moved, "ctx", 1)
        return (absorb(current, moved, (shard_spot - step_index - 1) * row_count), moved)

    running, packed_last = lax.fori_loop(0, REACH, advance_fixed, (running, packed_fwd))
    max_run, total_run, accum = running
    attended = (
        (accum / jnp.transpose(total_run, (2, 0, 1))[..., None])
        .reshape(row_count, HEADS * HEAD_DIM)
        .astype(jnp.bfloat16)
    )
    next_stream = from_behind(attended[None], "section", 1)
    upstream = from_behind(grad_held, "section", -1)
    out_grad = upstream[0].reshape(row_count, KV_HEADS, group_size, HEAD_DIM)
    lengths_bwd = doc_len_bwd[0]
    query_doc_bwd = doc_index(lengths_bwd, query_pos)
    queries_bwd = query_bwd[0].reshape(row_count, KV_HEADS, group_size, HEAD_DIM)
    packed_own = jnp.concatenate([key_bwd[0], value_bwd[0]], axis=1)
    stats_init = (
        jnp.full((KV_HEADS, group_size, row_count), MASKED_SCORE, jnp.float32),
        jnp.zeros((KV_HEADS, group_size, row_count), jnp.float32),
        jnp.zeros((KV_HEADS, group_size, row_count), jnp.float32),
    )

    def gather_stats(stats, piece_kv, first_row):
        allowed = piece_mask(lengths_bwd, query_doc_bwd, query_pos, first_row, piece_kv.shape[0])
        return stat_piece(stats, piece_kv, allowed, queries_bwd, out_grad, score_scale)

    move_keys = lambda moved: from_behind(moved, "ctx", 1)
    move_sums = lambda flowing: from_behind(flowing.astype(jnp.bfloat16), "ctx", -1).astype(
        flowing.dtype
    )
    stored = jnp.zeros((REACH + 1, row_count, 2 * kv_width), jnp.bfloat16)
    stored = lax.dynamic_update_slice(
        stored, packed_own[None], (jnp.int32(0), jnp.int32(0), jnp.int32(0))
    )
    stats = gather_stats(stats_init, packed_own, shard_spot * row_count)

    def collect(step_index, carry):
        current, moved, kept = carry
        moved = move_keys(moved)
        kept = lax.dynamic_update_slice(
            kept, moved[None], ((step_index + 1).astype(jnp.int32), jnp.int32(0), jnp.int32(0))
        )
        return (
            gather_stats(current, moved, (shard_spot - step_index - 1) * row_count),
            moved,
            kept,
        )

    stats, moved_last, stored = lax.fori_loop(0, REACH, collect, (stats, packed_own, stored))
    max_all, total_all, delta_run = stats
    delta_all = delta_run / total_all

    def piece_grads(offset):
        piece_kv = lax.dynamic_index_in_dim(stored, offset, 0, keepdims=False)
        first_row = (shard_spot - offset) * row_count
        allowed = piece_mask(lengths_bwd, query_doc_bwd, query_pos, first_row, row_count)
        return grad_piece(
            piece_kv, allowed, queries_bwd, out_grad, max_all, total_all, delta_all, score_scale
        )

    query_acc, carried_sum = piece_grads(REACH)

    def send_back(step_index, carry):
        query_now, flowing = carry
        offset = REACH - 1 - step_index
        flowing = move_sums(flowing)
        query_term, part = piece_grads(offset)
        return (query_now + query_term, flowing + part)

    query_acc, carried_sum = lax.fori_loop(0, REACH, send_back, (query_acc, carried_sum))
    grad_query = query_acc.reshape(row_count, HEADS * HEAD_DIM).astype(jnp.bfloat16)
    shares = carried_sum.astype(jnp.bfloat16)
    return (next_stream, grad_query[None], shares[:, :kv_width][None], shares[:, kv_width:][None])


def solution(mesh):
    in_specs = (
        P("section", "ctx", None),
        P("section", "ctx", None),
        P("section", "ctx", None),
        P("section", None),
        P("section", "ctx", None),
        P("section", "ctx", None),
        P("section", "ctx", None),
        P("section", None),
        P("section", "ctx", None),
    )
    out_specs = (
        P("section", "ctx", None),
        P("section", "ctx", None),
        P("section", "ctx", None),
        P("section", "ctx", None),
    )
    return jax.shard_map(
        on_device, mesh=mesh, in_specs=in_specs, out_specs=out_specs, check_vma=False
    )
```

profile of v0, /device:TPU:183, one launch (start us, length us, event | category | flops | bytes accessed | tf_op | source)
XLA Modules:
  0.0 189.9 jit_solution(8833590807049084600)
XLA Ops:
  0.7 2.4 %copy.300 = bf16[1,128,4096]{1,2,0:T(8,128)(2,1)} copy(bf16[1,128,4096]{2,1,0:T(8,128)(2,1)} %param.23) | data formatting | bytes 2097152 | tf_op args[8]
  3.0 2.4 %collective-permute-start.4 = (bf16[1,128,4096]{1,2,0:T(8,128)(2,1)}, bf16[1,128,4096]{1,2,0:T(8,128)(2,1)}, u32[]{:S(2)}, u32[]{:S(2)}) collective-permute-start(bf16[1,128,4096]{1,2,0:T(8,128)(2,1)} %copy.300), channel_id=1, source_target_pairs={{16,0},{32,16},{48,32},{64,48},{80,64},{96,80},{112,96},{128,112},... | collective-permute-start | bytes 3145736 | tf_op jit(solution)/shard_map/ppermute | solution.py:18
  8.1 0.9 and_and_fusion.3
  10.3 1.0 copy.274
  14.1 34.4 %while.64 = (s32[]{:T(128)}, f32[4,8,128]{2,1,0:T(8,128)S(1)}, f32[4,8,128]{2,1,0:T(8,128)S(1)}, f32[128,4,8,128]{3,0,2,1:T(8,128)S(1)}, bf16[128,1024]{0,1:T(8,...) while((s32[]{:T(128)}, f32[4,8,128]{2,1,0:T(8,128)S(1)}, ...), condition=%wide.region_21.22_spmd.clone, body=%wide.region_11.21_spmd.clone.sunk | while | flops 275888512 | bytes 18567700 | solution.py:188
  14.1 3.5 %collective-permute-start = (bf16[128,1024]{0,1:T(8,128)(2,1)}, bf16[128,1024]{0,1:T(8,128)(2,1)S(1)}, u32[]{:S(2)}, u32[]{:S(2)}) collective-permute-start(bf16[128,1024]{0,1:T(8,128)(2,1)} %get-tuple-element.1645), channel_id=1, source_target_pairs={{0,1},{1,2},{2,3},{3,4},{4,5},{5,6},{6,7},{7,8},{8,9},{9,10},{10,1... | collective-permute-start | bytes 786440 | tf_op jit(solution)/shard_map/while/body/eval_jaxpr/ppermute | solution.py:18
  17.9 3.4 %collective-permute-done = bf16[128,1024]{0,1:T(8,128)(2,1)S(1)} collective-permute-done((bf16[128,1024]{0,1:T(8,128)(2,1)}, bf16[128,1024]{0,1:T(8,128)(2,1)S(1)}, u32[]{:S(2)}, u32[]{:S(2)}) %collective-permute-start) | collective-permute-done | bytes 262176 | tf_op jit(solution)/shard_map/while/body/eval_jaxpr/ppermute | solution.py:18
  25.1 4.3 %collective-permute-start = (bf16[128,1024]{0,1:T(8,128)(2,1)}, bf16[128,1024]{0,1:T(8,128)(2,1)S(1)}, u32[]{:S(2)}, u32[]{:S(2)}) collective-permute-start(bf16[128,1024]{0,1:T(8,128)(2,1)} %get-tuple-element.1645), channel_id=1, source_target_pairs={{0,1},{1,2},{2,3},{3,4},{4,5},{5,6},{6,7},{7,8},{8,9},{9,10},{10,1... | collective-permute-start | bytes 786440 | tf_op jit(solution)/shard_map/while/body/eval_jaxpr/ppermute | solution.py:18
  29.6 3.4 %collective-permute-done = bf16[128,1024]{0,1:T(8,128)(2,1)S(1)} collective-permute-done((bf16[128,1024]{0,1:T(8,128)(2,1)}, bf16[128,1024]{0,1:T(8,128)(2,1)S(1)}, u32[]{:S(2)}, u32[]{:S(2)}) %collective-permute-start) | collective-permute-done | bytes 262176 | tf_op jit(solution)/shard_map/while/body/eval_jaxpr/ppermute | solution.py:18
  36.8 4.3 %collective-permute-start = (bf16[128,1024]{0,1:T(8,128)(2,1)}, bf16[128,1024]{0,1:T(8,128)(2,1)S(1)}, u32[]{:S(2)}, u32[]{:S(2)}) collective-permute-start(bf16[128,1024]{0,1:T(8,128)(2,1)} %get-tuple-element.1645), channel_id=1, source_target_pairs={{0,1},{1,2},{2,3},{3,4},{4,5},{5,6},{6,7},{7,8},{8,9},{9,10},{10,1... | collective-permute-start | bytes 786440 | tf_op jit(solution)/shard_map/while/body/eval_jaxpr/ppermute | solution.py:18
  41.3 3.4 %collective-permute-done = bf16[128,1024]{0,1:T(8,128)(2,1)S(1)} collective-permute-done((bf16[128,1024]{0,1:T(8,128)(2,1)}, bf16[128,1024]{0,1:T(8,128)(2,1)S(1)}, u32[]{:S(2)}, u32[]{:S(2)}) %collective-permute-start) | collective-permute-done | bytes 262176 | tf_op jit(solution)/shard_map/while/body/eval_jaxpr/ppermute | solution.py:18
  49.9 1.3 convert_element_type.274
  51.2 5.2 %collective-permute-start.3 = (bf16[1,128,4096]{2,1,0:T(8,128)(2,1)}, bf16[1,128,4096]{2,1,0:T(8,128)(2,1)}, u32[]{:S(2)}, u32[]{:S(2)}) collective-permute-start(bf16[1,128,4096]{2,1,0:T(8,128)(2,1)} %convert_element_type.274), channel_id=1, source_target_pairs={{0,16},{16,32},{32,48},{48,64},{64,80},{80,96},{96,112},{112,128},... | collective-permute-start | bytes 3145736 | tf_op jit(solution)/shard_map/ppermute | solution.py:18
  60.4 1.1 dynamic_update_slice.13
  62.6 1.6 copy.301
  64.2 1.3 fusion.266
  65.5 1.3 fusion.267
  67.5 36.3 %while.65 = (s32[]{:T(128)}, f32[4,8,128]{2,1,0:T(8,128)S(1)}, f32[4,8,128]{2,1,0:T(8,128)S(1)}, f32[4,8,128]{2,1,0:T(8,128)S(1)}, bf16[128,1024]{0,1:T(8,128)(2...) while((s32[]{:T(128)}, f32[4,8,128]{2,1,0:T(8,128)S(1)}, ...), condition=%wide.region_51.52_spmd.clone, body=%wide.region_37.51_spmd.clone.sunk | while | flops 273807744 | bytes 11850339 | solution.py:234
  67.5 4.6 %collective-permute-start.1 = (bf16[128,1024]{0,1:T(8,128)(2,1)}, bf16[128,1024]{0,1:T(8,128)(2,1)S(1)}, u32[]{:S(2)}, u32[]{:S(2)}) collective-permute-start(bf16[128,1024]{0,1:T(8,128)(2,1)} %get-tuple-element.1688), channel_id=1, source_target_pairs={{0,1},{1,2},{2,3},{3,4},{4,5},{5,6},{6,7},{7,8},{8,9},{9,10},{10,1... | collective-permute-start | bytes 786440 | tf_op jit(solution)/shard_map/while/body/eval_jaxpr/ppermute | solution.py:18
  73.6 2.1 %collective-permute-done.1 = bf16[128,1024]{0,1:T(8,128)(2,1)S(1)} collective-permute-done((bf16[128,1024]{0,1:T(8,128)(2,1)}, bf16[128,1024]{0,1:T(8,128)(2,1)S(1)}, u32[]{:S(2)}, u32[]{:S(2)}) %collective-permute-start.1) | collective-permute-done | bytes 262176 | tf_op jit(solution)/shard_map/while/body/eval_jaxpr/ppermute | solution.py:18
  79.8 4.3 %collective-permute-start.1 = (bf16[128,1024]{0,1:T(8,128)(2,1)}, bf16[128,1024]{0,1:T(8,128)(2,1)S(1)}, u32[]{:S(2)}, u32[]{:S(2)}) collective-permute-start(bf16[128,1024]{0,1:T(8,128)(2,1)} %get-tuple-element.1688), channel_id=1, source_target_pairs={{0,1},{1,2},{2,3},{3,4},{4,5},{5,6},{6,7},{7,8},{8,9},{9,10},{10,1... | collective-permute-start | bytes 786440 | tf_op jit(solution)/shard_map/while/body/eval_jaxpr/ppermute | solution.py:18
  85.6 2.1 %collective-permute-done.1 = bf16[128,1024]{0,1:T(8,128)(2,1)S(1)} collective-permute-done((bf16[128,1024]{0,1:T(8,128)(2,1)}, bf16[128,1024]{0,1:T(8,128)(2,1)S(1)}, u32[]{:S(2)}, u32[]{:S(2)}) %collective-permute-start.1) | collective-permute-done | bytes 262176 | tf_op jit(solution)/shard_map/while/body/eval_jaxpr/ppermute | solution.py:18
  91.8 4.3 %collective-permute-start.1 = (bf16[128,1024]{0,1:T(8,128)(2,1)}, bf16[128,1024]{0,1:T(8,128)(2,1)S(1)}, u32[]{:S(2)}, u32[]{:S(2)}) collective-permute-start(bf16[128,1024]{0,1:T(8,128)(2,1)} %get-tuple-element.1688), channel_id=1, source_target_pairs={{0,1},{1,2},{2,3},{3,4},{4,5},{5,6},{6,7},{7,8},{8,9},{9,10},{10,1... | collective-permute-start | bytes 786440 | tf_op jit(solution)/shard_map/while/body/eval_jaxpr/ppermute | solution.py:18
  97.6 2.1 %collective-permute-done.1 = bf16[128,1024]{0,1:T(8,128)(2,1)S(1)} collective-permute-done((bf16[128,1024]{0,1:T(8,128)(2,1)}, bf16[128,1024]{0,1:T(8,128)(2,1)S(1)}, u32[]{:S(2)}, u32[]{:S(2)}) %collective-permute-start.1) | collective-permute-done | bytes 262176 | tf_op jit(solution)/shard_map/while/body/eval_jaxpr/ppermute | solution.py:18
  103.8 1.0 slice_bitcast_fusion.80
  111.2 1.5 pad_maximum_fusion.9
  112.7 70.1 %while.66 = (s32[]{:T(128)}, f32[128,4,8,128]{0,3,2,1:T(8,128)}, bf16[128,1024]{0,1:T(8,128)(2,1)}, bf16[4,128,1024]{1,2,0:T(8,128)(2,1)}, s32[128]{0:T(128)}, /...) while((s32[]{:T(128)}, f32[128,4,8,128]{0,3,2,1:T(8,128)}, ...), condition=%wide.region_55.56_spmd.clone, body=%wide.region_53.55_spmd.clone.sunk | while | flops 680008064 | bytes 26579668 | solution.py:255
  112.7 3.6 %collective-permute-start.2 = (bf16[128,1024]{0,1:T(8,128)(2,1)}, bf16[128,1024]{0,1:T(8,128)(2,1)S(1)}, u32[]{:S(2)}, u32[]{:S(2)}) collective-permute-start(bf16[128,1024]{0,1:T(8,128)(2,1)} %get-tuple-element.1738), channel_id=1, source_target_pairs={{1,0},{2,1},{3,2},{4,3},{5,4},{6,5},{7,6},{8,7},{9,8},{10,9},{11,1... | collective-permute-start | bytes 786440 | tf_op jit(solution)/shard_map/while/body/eval_jaxpr/ppermute | solution.py:18
  116.4 1.0 dynamic-slice_bitcast_fusion.2
  122.0 0.9 fusion.524
  123.2 0.9 fusion.528
  124.0 1.0 fusion.520
  125.4 0.9 fusion.521
  126.5 0.9 fusion.525
  127.4 1.0 fusion.511
  128.4 0.8 pad_maximum_fusion.34
  129.2 0.8 pad_maximum_fusion.33
  130.1 3.5 %maximum_add_fusion.2 = f32[128,4,8,128]{0,3,2,1:T(8,128)} fusion(f32[128,4,8,128]{0,3,2,1:T(8,128)} %get-tuple-element.1737, f32[128,1,8,128]{0,3,2,1:T(8,128)} %fusion.511, f32[128,1,8,128]{0,3,2,1:T(8,128)S(1)} %fusion.514, f32[128,1,8,128]{0,3,2,1:T(8,128)S(1)} %fusion.517, f32[128,1,8,128]{0,3,2,1:T(8,128)} %fusion.520), kind=kLoop, calls=%fused_computation.192.clone.1 | loop fusion | flops 2097152 | bytes 6291456 | tf_op jit(solution)/shard_map/while/body/eval_jaxpr/add | solution.py:253
  134.4 4.3 %collective-permute-start.2 = (bf16[128,1024]{0,1:T(8,128)(2,1)}, bf16[128,1024]{0,1:T(8,128)(2,1)S(1)}, u32[]{:S(2)}, u32[]{:S(2)}) collective-permute-start(bf16[128,1024]{0,1:T(8,128)(2,1)} %get-tuple-element.1738), channel_id=1, source_target_pairs={{1,0},{2,1},{3,2},{4,3},{5,4},{6,5},{7,6},{8,7},{9,8},{10,9},{11,1... | collective-permute-start | bytes 786440 | tf_op jit(solution)/shard_map/while/body/eval_jaxpr/ppermute | solution.py:18
  138.8 1.0 dynamic-slice_bitcast_fusion.2
  144.4 0.9 fusion.524
  145.6 0.9 fusion.528
  146.5 1.0 fusion.520
  147.8 0.9 fusion.521
  149.0 0.9 fusion.525
  149.9 1.0 fusion.511
  150.9 0.8 pad_maximum_fusion.34
  151.7 0.8 pad_maximum_fusion.33
  152.5 3.5 %maximum_add_fusion.2 = f32[128,4,8,128]{0,3,2,1:T(8,128)} fusion(f32[128,4,8,128]{0,3,2,1:T(8,128)} %get-tuple-element.1737, f32[128,1,8,128]{0,3,2,1:T(8,128)} %fusion.511, f32[128,1,8,128]{0,3,2,1:T(8,128)S(1)} %fusion.514, f32[128,1,8,128]{0,3,2,1:T(8,128)S(1)} %fusion.517, f32[128,1,8,128]{0,3,2,1:T(8,128)} %fusion.520), kind=kLoop, calls=%fused_computation.192.clone.1 | loop fusion | flops 2097152 | bytes 6291456 | tf_op jit(solution)/shard_map/while/body/eval_jaxpr/add | solution.py:253
  156.8 7.9 %collective-permute-start.2 = (bf16[128,1024]{0,1:T(8,128)(2,1)}, bf16[128,1024]{0,1:T(8,128)(2,1)S(1)}, u32[]{:S(2)}, u32[]{:S(2)}) collective-permute-start(bf16[128,1024]{0,1:T(8,128)(2,1)} %get-tuple-element.1738), channel_id=1, source_target_pairs={{1,0},{2,1},{3,2},{4,3},{5,4},{6,5},{7,6},{8,7},{9,8},{10,9},{11,1... | collective-permute-start | bytes 786440 | tf_op jit(solution)/shard_map/while/body/eval_jaxpr/ppermute | solution.py:18
  164.7 1.0 dynamic-slice_bitcast_fusion.2
  170.4 0.9 fusion.524
  171.5 0.9 fusion.528
  172.4 1.0 fusion.520
  173.7 0.9 fusion.521
  174.9 0.9 fusion.525
  175.8 1.0 fusion.511
  176.8 0.8 pad_maximum_fusion.34
  177.6 0.8 pad_maximum_fusion.33
  178.4 3.5 %maximum_add_fusion.2 = f32[128,4,8,128]{0,3,2,1:T(8,128)} fusion(f32[128,4,8,128]{0,3,2,1:T(8,128)} %get-tuple-element.1737, f32[128,1,8,128]{0,3,2,1:T(8,128)} %fusion.511, f32[128,1,8,128]{0,3,2,1:T(8,128)S(1)} %fusion.514, f32[128,1,8,128]{0,3,2,1:T(8,128)S(1)} %fusion.517, f32[128,1,8,128]{0,3,2,1:T(8,128)} %fusion.520), kind=kLoop, calls=%fused_computation.192.clone.1 | loop fusion | flops 2097152 | bytes 6291456 | tf_op jit(solution)/shard_map/while/body/eval_jaxpr/add | solution.py:253
  182.7 1.8 convert_element_type.286
  184.5 1.3 copy.408
  185.8 1.1 copy.347
  187.6 2.3 %copy.505 = bf16[1,128,4096]{2,1,0:T(8,128)(2,1)} copy(bf16[1,128,4096]{2,1,0:T(8,128)(2,1)} %collective-permute-done.3) | data formatting | bytes 2097152
  (331 shorter events, 67.2 us)
Async XLA Ops:
  0.6 4.9 %copy-start.11 = (s32[1,16]{1,0:T(1,128)S(1)}, s32[1,16]{1,0:T(1,128)}, u32[]{:S(2)}) copy-start(s32[1,16]{1,0:T(1,128)} %param.18) | copy-start | bytes 196
  0.6 5.1 %copy-start.12 = (s32[1,16]{1,0:T(1,128)S(1)}, s32[1,16]{1,0:T(1,128)}, u32[]{:S(2)}) copy-start(s32[1,16]{1,0:T(1,128)} %param.22) | copy-start | bytes 196
  0.7 5.3 %copy-start.4 = (bf16[1,128,4096]{2,1,0:T(8,128)(2,1)S(1)}, bf16[1,128,4096]{2,1,0:T(8,128)(2,1)}, u32[]{:S(2)}) copy-start(bf16[1,128,4096]{2,1,0:T(8,128)(2,1)} %param.15) | copy-start | bytes 3145732
  3.0 59.3 %collective-permute-start.4 = (bf16[1,128,4096]{1,2,0:T(8,128)(2,1)}, bf16[1,128,4096]{1,2,0:T(8,128)(2,1)}, u32[]{:S(2)}, u32[]{:S(2)}) collective-permute-start(bf16[1,128,4096]{1,2,0:T(8,128)(2,1)} %copy.300), channel_id=1, source_target_pairs={{16,0},{32,16},{48,32},{64,48},{80,64},{96,80},{112,96},{128,112},... | collective-permute-start | bytes 3145736 | tf_op jit(solution)/shard_map/ppermute | solution.py:18
  6.0 1.4 copy-start.8
  14.1 7.1 %collective-permute-start = (bf16[128,1024]{0,1:T(8,128)(2,1)}, bf16[128,1024]{0,1:T(8,128)(2,1)S(1)}, u32[]{:S(2)}, u32[]{:S(2)}) collective-permute-start(bf16[128,1024]{0,1:T(8,128)(2,1)} %get-tuple-element.1645), channel_id=1, source_target_pairs={{0,1},{1,2},{2,3},{3,4},{4,5},{5,6},{6,7},{7,8},{8,9},{9,10},{10,1... | collective-permute-start | bytes 786440 | tf_op jit(solution)/shard_map/while/body/eval_jaxpr/ppermute | solution.py:18
  25.1 7.9 %collective-permute-start = (bf16[128,1024]{0,1:T(8,128)(2,1)}, bf16[128,1024]{0,1:T(8,128)(2,1)S(1)}, u32[]{:S(2)}, u32[]{:S(2)}) collective-permute-start(bf16[128,1024]{0,1:T(8,128)(2,1)} %get-tuple-element.1645), channel_id=1, source_target_pairs={{0,1},{1,2},{2,3},{3,4},{4,5},{5,6},{6,7},{7,8},{8,9},{9,10},{10,1... | collective-permute-start | bytes 786440 | tf_op jit(solution)/shard_map/while/body/eval_jaxpr/ppermute | solution.py:18
  36.8 7.9 %collective-permute-start = (bf16[128,1024]{0,1:T(8,128)(2,1)}, bf16[128,1024]{0,1:T(8,128)(2,1)S(1)}, u32[]{:S(2)}, u32[]{:S(2)}) collective-permute-start(bf16[128,1024]{0,1:T(8,128)(2,1)} %get-tuple-element.1645), channel_id=1, source_target_pairs={{0,1},{1,2},{2,3},{3,4},{4,5},{5,6},{6,7},{7,8},{8,9},{9,10},{10,1... | collective-permute-start | bytes 786440 | tf_op jit(solution)/shard_map/while/body/eval_jaxpr/ppermute | solution.py:18
  49.2 7.2 %copy-start.5 = (bf16[1,128,4096]{2,1,0:T(8,128)(2,1)S(1)}, bf16[1,128,4096]{2,1,0:T(8,128)(2,1)}, u32[]{:S(2)}) copy-start(bf16[1,128,4096]{2,1,0:T(8,128)(2,1)} %param.19) | copy-start | bytes 3145732
  51.2 6.6 %copy-start.9 = (bf16[1,128,512]{2,1,0:T(8,128)(2,1)S(1)}, bf16[1,128,512]{2,1,0:T(8,128)(2,1)}, u32[]{:S(2)}) copy-start(bf16[1,128,512]{2,1,0:T(8,128)(2,1)} %param.20) | copy-start | bytes 393220
  51.2 136.4 %collective-permute-start.3 = (bf16[1,128,4096]{2,1,0:T(8,128)(2,1)}, bf16[1,128,4096]{2,1,0:T(8,128)(2,1)}, u32[]{:S(2)}, u32[]{:S(2)}) collective-permute-start(bf16[1,128,4096]{2,1,0:T(8,128)(2,1)} %convert_element_type.274), channel_id=1, source_target_pairs={{0,16},{16,32},{32,48},{48,64},{64,80},{80,96},{96,112},{112,128},... | collective-permute-start | bytes 3145736 | tf_op jit(solution)/shard_map/ppermute | solution.py:18
  57.8 1.0 copy-start.10
  58.8 3.5 %copy-start.2 = (f32[8,128,128]{1,2,0:T(8,128)}, f32[8,128,128]{1,2,0:T(8,128)S(1)}, u32[]{:S(2)}) copy-start(f32[8,128,128]{1,2,0:T(8,128)S(1)} %get-tuple-element.1252) | copy-start | bytes 1572868
  61.8 0.8 copy-start.3
  67.5 8.2 %collective-permute-start.1 = (bf16[128,1024]{0,1:T(8,128)(2,1)}, bf16[128,1024]{0,1:T(8,128)(2,1)S(1)}, u32[]{:S(2)}, u32[]{:S(2)}) collective-permute-start(bf16[128,1024]{0,1:T(8,128)(2,1)} %get-tuple-element.1688), channel_id=1, source_target_pairs={{0,1},{1,2},{2,3},{3,4},{4,5},{5,6},{6,7},{7,8},{8,9},{9,10},{10,1... | collective-permute-start | bytes 786440 | tf_op jit(solution)/shard_map/while/body/eval_jaxpr/ppermute | solution.py:18
  79.8 7.9 %collective-permute-start.1 = (bf16[128,1024]{0,1:T(8,128)(2,1)}, bf16[128,1024]{0,1:T(8,128)(2,1)S(1)}, u32[]{:S(2)}, u32[]{:S(2)}) collective-permute-start(bf16[128,1024]{0,1:T(8,128)(2,1)} %get-tuple-element.1688), channel_id=1, source_target_pairs={{0,1},{1,2},{2,3},{3,4},{4,5},{5,6},{6,7},{7,8},{8,9},{9,10},{10,1... | collective-permute-start | bytes 786440 | tf_op jit(solution)/shard_map/while/body/eval_jaxpr/ppermute | solution.py:18
  91.8 7.9 %collective-permute-start.1 = (bf16[128,1024]{0,1:T(8,128)(2,1)}, bf16[128,1024]{0,1:T(8,128)(2,1)S(1)}, u32[]{:S(2)}, u32[]{:S(2)}) collective-permute-start(bf16[128,1024]{0,1:T(8,128)(2,1)} %get-tuple-element.1688), channel_id=1, source_target_pairs={{0,1},{1,2},{2,3},{3,4},{4,5},{5,6},{6,7},{7,8},{8,9},{9,10},{10,1... | collective-permute-start | bytes 786440 | tf_op jit(solution)/shard_map/while/body/eval_jaxpr/ppermute | solution.py:18
  112.7 6.6 %copy-start = (f32[4,8,128]{2,1,0:T(8,128)}, f32[4,8,128]{2,1,0:T(8,128)S(1)}, u32[]{:S(2)}) copy-start(f32[4,8,128]{2,1,0:T(8,128)S(1)} %get-tuple-element.1763) | copy-start | bytes 49156 | tf_op jit(solution)/shard_map/while
  112.7 6.6 %copy-start.6 = (f32[4,8,128]{2,1,0:T(8,128)}, f32[4,8,128]{2,1,0:T(8,128)S(1)}, u32[]{:S(2)}) copy-start(f32[4,8,128]{2,1,0:T(8,128)S(1)} %get-tuple-element.1765) | copy-start | bytes 49156 | tf_op jit(solution)/shard_map/while
  112.7 20.9 %collective-permute-start.2 = (bf16[128,1024]{0,1:T(8,128)(2,1)}, bf16[128,1024]{0,1:T(8,128)(2,1)S(1)}, u32[]{:S(2)}, u32[]{:S(2)}) collective-permute-start(bf16[128,1024]{0,1:T(8,128)(2,1)} %get-tuple-element.1738), channel_id=1, source_target_pairs={{1,0},{2,1},{3,2},{4,3},{5,4},{6,5},{7,6},{8,7},{9,8},{10,9},{11,1... | collective-permute-start | bytes 786440 | tf_op jit(solution)/shard_map/while/body/eval_jaxpr/ppermute | solution.py:18
  130.0 4.3 %copy-start.1 = (f32[4,8,128]{2,1,0:T(8,128)S(1)}, f32[4,8,128]{2,1,0:T(8,128)}, u32[]{:S(2)}) copy-start(f32[4,8,128]{2,1,0:T(8,128)} %copy-done) | copy-start | bytes 49156 | tf_op jit(solution)/shard_map/while
  130.0 4.3 %copy-start.7 = (f32[4,8,128]{2,1,0:T(8,128)S(1)}, f32[4,8,128]{2,1,0:T(8,128)}, u32[]{:S(2)}) copy-start(f32[4,8,128]{2,1,0:T(8,128)} %copy-done.6) | copy-start | bytes 49156 | tf_op jit(solution)/shard_map/while
  134.4 7.3 %copy-start = (f32[4,8,128]{2,1,0:T(8,128)}, f32[4,8,128]{2,1,0:T(8,128)S(1)}, u32[]{:S(2)}) copy-start(f32[4,8,128]{2,1,0:T(8,128)S(1)} %get-tuple-element.1763) | copy-start | bytes 49156 | tf_op jit(solution)/shard_map/while
  134.4 7.3 %copy-start.6 = (f32[4,8,128]{2,1,0:T(8,128)}, f32[4,8,128]{2,1,0:T(8,128)S(1)}, u32[]{:S(2)}) copy-start(f32[4,8,128]{2,1,0:T(8,128)S(1)} %get-tuple-element.1765) | copy-start | bytes 49156 | tf_op jit(solution)/shard_map/while
  134.4 21.6 %collective-permute-start.2 = (bf16[128,1024]{0,1:T(8,128)(2,1)}, bf16[128,1024]{0,1:T(8,128)(2,1)S(1)}, u32[]{:S(2)}, u32[]{:S(2)}) collective-permute-start(bf16[128,1024]{0,1:T(8,128)(2,1)} %get-tuple-element.1738), channel_id=1, source_target_pairs={{1,0},{2,1},{3,2},{4,3},{5,4},{6,5},{7,6},{8,7},{9,8},{10,9},{11,1... | collective-permute-start | bytes 786440 | tf_op jit(solution)/shard_map/while/body/eval_jaxpr/ppermute | solution.py:18
  152.5 4.3 %copy-start.1 = (f32[4,8,128]{2,1,0:T(8,128)S(1)}, f32[4,8,128]{2,1,0:T(8,128)}, u32[]{:S(2)}) copy-start(f32[4,8,128]{2,1,0:T(8,128)} %copy-done) | copy-start | bytes 49156 | tf_op jit(solution)/shard_map/while
  152.5 4.3 %copy-start.7 = (f32[4,8,128]{2,1,0:T(8,128)S(1)}, f32[4,8,128]{2,1,0:T(8,128)}, u32[]{:S(2)}) copy-start(f32[4,8,128]{2,1,0:T(8,128)} %copy-done.6) | copy-start | bytes 49156 | tf_op jit(solution)/shard_map/while
  156.8 10.8 %copy-start = (f32[4,8,128]{2,1,0:T(8,128)}, f32[4,8,128]{2,1,0:T(8,128)S(1)}, u32[]{:S(2)}) copy-start(f32[4,8,128]{2,1,0:T(8,128)S(1)} %get-tuple-element.1763) | copy-start | bytes 49156 | tf_op jit(solution)/shard_map/while
  156.8 10.8 %copy-start.6 = (f32[4,8,128]{2,1,0:T(8,128)}, f32[4,8,128]{2,1,0:T(8,128)S(1)}, u32[]{:S(2)}) copy-start(f32[4,8,128]{2,1,0:T(8,128)S(1)} %get-tuple-element.1765) | copy-start | bytes 49156 | tf_op jit(solution)/shard_map/while
  156.8 25.1 %collective-permute-start.2 = (bf16[128,1024]{0,1:T(8,128)(2,1)}, bf16[128,1024]{0,1:T(8,128)(2,1)S(1)}, u32[]{:S(2)}, u32[]{:S(2)}) collective-permute-start(bf16[128,1024]{0,1:T(8,128)(2,1)} %get-tuple-element.1738), channel_id=1, source_target_pairs={{1,0},{2,1},{3,2},{4,3},{5,4},{6,5},{7,6},{8,7},{9,8},{10,9},{11,1... | collective-permute-start | bytes 786440 | tf_op jit(solution)/shard_map/while/body/eval_jaxpr/ppermute | solution.py:18
  178.4 4.3 %copy-start.1 = (f32[4,8,128]{2,1,0:T(8,128)S(1)}, f32[4,8,128]{2,1,0:T(8,128)}, u32[]{:S(2)}) copy-start(f32[4,8,128]{2,1,0:T(8,128)} %copy-done) | copy-start | bytes 49156 | tf_op jit(solution)/shard_map/while
  178.4 4.3 %copy-start.7 = (f32[4,8,128]{2,1,0:T(8,128)S(1)}, f32[4,8,128]{2,1,0:T(8,128)}, u32[]{:S(2)}) copy-start(f32[4,8,128]{2,1,0:T(8,128)} %copy-done.6) | copy-start | bytes 49156 | tf_op jit(solution)/shard_map/while
where the time goes:
time: 191 us; the launch traced here: 190 us
  matrix products  53.5 us (28%)
  starting transfers between devices  48.7 us (25%)
  other arithmetic  41.1 us (22%)
  local copies, waits for them, and re-layouts  27.5 us (14%)
  waiting for transfers between devices  16.4 us (9%)
    ppermute x11, starting transfers between devices, from_behind(): lax.ppermute(value, axis, [(source, source + steps) for source in range(f...  48.7 us
    ppermute x11, waiting for transfers between devices, from_behind(): lax.ppermute(value, axis, [(source, source + steps) for source in range(f...  16.4 us
    add x6, other arithmetic, send_back(): return (query_now + query_term, flowing + part)  12.9 us
    dot_general x16, matrix products, grad_piece(): jnp.einsum('hqk,kd->qhd', d_score, key_rows[:, kv_group], preferred_eleme...  8.26 us
    dot_general x16, matrix products, grad_piece(): jnp.einsum('hqk,qhd->kd', low_probs, out_grad[:, kv_group], preferred_ele...  8.25 us
    dot_general x16, matrix products, grad_piece(): jnp.einsum('hqk,qhd->kd', d_score, queries[:, kv_group], preferred_elemen...  8.1 us
    unnamed x26, local copies, waits for them, and re-layouts  7.72 us
    dot_general x16, matrix products, stat_piece(): jnp.einsum('qhd,kd->hqk', out_grad[:, kv_group], value_rows[:, kv_group],...  6.27 us
  transfers between devices with their start and end apart: 11, of which 6 were waited for; matrix products, arithmetic and copies ran while one was open for 62% of the time, Pallas kernels for 0%

commit v1 on v0

v1 whole, which is shorter than its diff:
```python
import math

import jax
import jax.numpy as jnp
from jax import lax
from jax.experimental import pallas as pl
from jax.experimental.pallas import tpu as pltpu
from jax.sharding import PartitionSpec as P

HEADS = 32
KV_HEADS = 4
GROUP = HEADS // KV_HEADS
HEAD_DIM = 128
REACH = 3
ROWS = 128
KEYS = (REACH + 1) * ROWS
DOCS = 16
SCALE = HEAD_DIM**-0.5
SCALE_LOG2 = SCALE * math.log2(math.e)
MASKED = -1e30
KV_WIDTH = KV_HEADS * HEAD_DIM
GROUP_WIDTH = GROUP * HEAD_DIM
CHUNKS = (2, 2)
VMEM = 48 * 1024 * 1024
NT = (((1,), (1,)), ((), ()))


def from_behind(value, axis, steps, what="moved"):
    count = lax.axis_size(axis)
    with jax.named_scope(what):
        return lax.ppermute(value, axis, [(at, (at + steps) % count) for at in range(count)])


def after(*values):
    return lax.optimization_barrier(values)


def params():
    return pltpu.CompilerParams(vmem_limit_bytes=VMEM)


def cost(flops, bytes_accessed):
    return pl.CostEstimate(flops=flops, bytes_accessed=bytes_accessed, transcendentals=0)


def fill_bias(place_ref, len_ref, bias_ref):
    base = (place_ref[0] - REACH) * ROWS
    key = base + lax.broadcasted_iota(jnp.int32, (KEYS, ROWS), 0)
    query = base + REACH * ROWS + lax.broadcasted_iota(jnp.int32, (8, ROWS), 1)
    start = jnp.zeros((8, ROWS), jnp.int32)
    end = jnp.int32(0)
    for doc in range(DOCS):
        end = end + len_ref[0, doc]
        start = jnp.where(query >= end, end, start)
    bias = jnp.where((key >= start[:1]) & (key <= query[:1]), 0.0, MASKED)
    bias_ref[:, :ROWS] = bias
    bias_ref[:, ROWS:] = bias


def two_heads(ref, pair):
    at = 2 * pair * HEAD_DIM
    return jnp.concatenate(
        [ref[0, :, at : at + HEAD_DIM], ref[0, :, at + HEAD_DIM : at + 2 * HEAD_DIM]], axis=0
    )


def weights_of(keys, queries, bias_ref):
    scores = lax.dot_general(keys, queries, NT, preferred_element_type=jnp.float32)
    scores = scores + bias_ref[...]
    top = jnp.max(scores, axis=0, keepdims=True)
    weights = jnp.exp2((scores - top) * SCALE_LOG2)
    return weights, 1.0 / jnp.sum(weights, axis=0, keepdims=True)


def put_heads(out_ref, pair, flipped):
    at = 2 * pair * HEAD_DIM
    out_ref[0, :, at : at + HEAD_DIM] = flipped[:, :ROWS].T.astype(jnp.bfloat16)
    out_ref[0, :, at + HEAD_DIM : at + 2 * HEAD_DIM] = flipped[:, ROWS:].T.astype(jnp.bfloat16)


def stacked(refs):
    return jnp.concatenate([ref[0] for ref in refs], axis=0)


def forward_kernel(place_ref, len_ref, query_ref, *refs):
    key_refs, value_refs, (out_ref, bias_ref) = refs[:4], refs[4:8], refs[8:]

    @pl.when(pl.program_id(0) == 0)
    def _():
        fill_bias(place_ref, len_ref, bias_ref)

    keep = place_ref[1].astype(jnp.float32)
    keys = stacked(key_refs)
    values_t = stacked(value_refs).T
    for pair in range(GROUP // 2):
        weights, inverse = weights_of(keys, two_heads(query_ref, pair), bias_ref)
        mixed = jnp.dot(
            values_t, weights.astype(jnp.bfloat16), preferred_element_type=jnp.float32
        )
        put_heads(out_ref, pair, mixed * (inverse * keep))


def backward_kernel(place_ref, len_ref, query_ref, grad_ref, *refs):
    key_refs, value_refs = refs[:4], refs[4:8]
    out_ref, own_ref, middle_ref, pair_ref, bias_ref = refs[-5:]

    @pl.when(pl.program_id(0) == 0)
    def _():
        fill_bias(place_ref, len_ref, bias_ref)

    keep = place_ref[2].astype(jnp.bfloat16)
    keys, values = stacked(key_refs), stacked(value_refs)
    keys_t = keys.T
    key_sum = value_sum = None
    for pair in range(GROUP // 2):
        queries, grads = two_heads(query_ref, pair), two_heads(grad_ref, pair) * keep
        weights, inverse = weights_of(keys, queries, bias_ref)
        d_prob = lax.dot_general(values, grads, NT, preferred_element_type=jnp.float32)
        probs = weights * inverse
        delta = jnp.sum(probs * d_prob, axis=0, keepdims=True)
        d_score = (probs * (d_prob - delta)).astype(jnp.bfloat16)
        key_term = jnp.dot(d_score, queries, preferred_element_type=jnp.float32)
        value_term = jnp.dot(
            probs.astype(jnp.bfloat16), grads, preferred_element_type=jnp.float32
        )
        key_sum = key_term if key_sum is None else key_sum + key_term
        value_sum = value_term if value_sum is None else value_sum + value_term
        d_query = jnp.dot(keys_t, d_score, preferred_element_type=jnp.float32)
        put_heads(out_ref, pair, d_query * SCALE)
    places = ((pair_ref, 1), (middle_ref, 0), (pair_ref, 0), (own_ref, 0))
    for piece, (part_ref, lead) in enumerate(places):
        at = slice(piece * ROWS, (piece + 1) * ROWS)
        part_ref[lead, :, :HEAD_DIM] = (key_sum[at] * SCALE).astype(jnp.bfloat16)
        part_ref[lead, :, HEAD_DIM:] = value_sum[at].astype(jnp.bfloat16)


def group_spec(first):
    return pl.BlockSpec((1, ROWS, GROUP_WIDTH), lambda i: (0, 0, first + i))


def common_specs(first):
    smem = pl.BlockSpec(memory_space=pltpu.SMEM)
    specs = []
    for col in (first, KV_HEADS + first):
        for lead in (1, 0, 0, 0):
            specs.append(
                pl.BlockSpec(
                    (1, ROWS, HEAD_DIM), lambda i, lead=lead, col=col: (lead, 0, col + i)
                )
            )
    return [smem, smem], specs


def in_order(own, middle, pair):
    return [pair, middle, pair, own] * 2


def forward(place, lengths, query, pieces):
    scalars, heads = common_specs(0)
    return pl.pallas_call(
        forward_kernel,
        grid=(KV_HEADS,),
        out_shape=jax.ShapeDtypeStruct(query.shape, jnp.bfloat16),
        in_specs=scalars + [group_spec(0)] + heads,
        out_specs=group_spec(0),
        scratch_shapes=[pltpu.VMEM((KEYS, 2 * ROWS), jnp.float32)],
        cost_estimate=cost(4 * HEADS * ROWS * KEYS * HEAD_DIM, 3 << 20),
        compiler_params=params(),
    )(place, lengths, query, *in_order(*pieces))


def backward(place, lengths, query, out_grad, pieces, first, so_far):
    groups = out_grad.shape[2] // GROUP_WIDTH
    width = groups * 2 * HEAD_DIM
    leads = (1, 1, 2)
    scalars, heads = common_specs(first)
    in_specs = scalars + [group_spec(first), group_spec(0)] + heads
    operands = [place, lengths, query, out_grad, *in_order(*pieces)]
    aliases = {}
    if so_far is not None:
        in_specs.append(pl.BlockSpec(memory_space=pl.ANY))
        aliases = {len(operands): 0}
        operands.append(so_far)
    result = pl.pallas_call(
        backward_kernel,
        grid=(groups,),
        out_shape=[jax.ShapeDtypeStruct(query.shape, jnp.bfloat16)]
        + [jax.ShapeDtypeStruct((lead, ROWS, width), jnp.bfloat16) for lead in leads],
        in_specs=in_specs,
        out_specs=[group_spec(first)]
        + [pl.BlockSpec((lead, ROWS, 2 * HEAD_DIM), lambda i: (0, 0, i)) for lead in leads],
        scratch_shapes=[pltpu.VMEM((KEYS, 2 * ROWS), jnp.float32)],
        input_output_aliases=aliases,
        cost_estimate=cost(10 * groups * GROUP * ROWS * KEYS * HEAD_DIM, groups << 20),
        compiler_params=params(),
    )(*operands)
    return result[0], result[1:]


def add_kernel(*refs):
    part_refs, (key_ref, value_ref) = refs[:-2], refs[-2:]
    first = 0
    for chunk, groups in enumerate(CHUNKS):
        total = part_refs[3 * chunk][0].astype(jnp.float32)
        for ref in part_refs[3 * chunk + 1 : 3 * chunk + 3]:
            total = total + ref[0].astype(jnp.float32)
        total = total.astype(jnp.bfloat16)
        for group in range(groups):
            at, to = 2 * group * HEAD_DIM, (first + group) * HEAD_DIM
            key_ref[0, :, to : to + HEAD_DIM] = total[:, at : at + HEAD_DIM]
            value_ref[0, :, to : to + HEAD_DIM] = total[:, at + HEAD_DIM : at + 2 * HEAD_DIM]
        first += groups


def add_parts(parts):
    shape = jax.ShapeDtypeStruct((1, ROWS, KV_WIDTH), jnp.bfloat16)
    return pl.pallas_call(
        add_kernel,
        out_shape=[shape, shape],
        grid=(1,),
        in_specs=[
            pl.BlockSpec((1,) + part.shape[1:], lambda i: (0, 0, 0)) for part in parts
        ],
        out_specs=[pl.BlockSpec(shape.shape, lambda i: (0, 0, 0))] * 2,
        cost_estimate=cost(0, 2 << 20),
        compiler_params=params(),
    )(*parts)


def on_device(
    query_fwd,
    key_fwd,
    value_fwd,
    doc_len_fwd,
    query_bwd,
    key_bwd,
    value_bwd,
    doc_len_bwd,
    grad_held,
):
    section = lax.axis_index("section")
    last = lax.axis_size("section") - 1
    place = jnp.stack([lax.axis_index("ctx"), section > 0, section < last]).astype(jnp.int32)
    starts = [sum(CHUNKS[:chunk]) for chunk in range(len(CHUNKS) + 1)]
    grads = [
        grad_held[:, :, at * GROUP_WIDTH : to * GROUP_WIDTH]
        for at, to in zip(starts[:-1], starts[1:])
    ]
    key_fwd, key_bwd, grads[0] = after(key_fwd, key_bwd, grads[0])
    out_grads = [
        from_behind(grad, "section", -1, f"grad_{chunk}") for chunk, grad in enumerate(grads)
    ]
    own_fwd = from_behind(
        jnp.concatenate([key_fwd, value_fwd], axis=2), "section", 1, "kv_moved"
    )
    len_moved = from_behind(doc_len_fwd, "section", 1, "len_moved")
    own_bwd = jnp.concatenate([key_bwd, value_bwd], axis=2)
    middle_bwd = from_behind(own_bwd, "ctx", 2, "kv_bwd_middle")
    query_fwd, own_fwd, len_moved = after(query_fwd, own_fwd, len_moved)
    query_moved = from_behind(query_fwd, "section", 1, "query_moved")
    middle_fwd = from_behind(own_fwd, "ctx", 2, "kv_fwd_middle")
    pair_bwd = from_behind(
        jnp.concatenate([own_bwd, middle_bwd], axis=0), "ctx", 1, "kv_bwd_pair"
    )
    middle_fwd, pair_bwd = after(middle_fwd, pair_bwd)
    pair_fwd = from_behind(
        jnp.concatenate([own_fwd, middle_fwd], axis=0), "ctx", 1, "kv_fwd_pair"
    )
    grad_query = None
    parts = []
    for chunk, out_grad in enumerate(out_grads):
        grad_query, (own, middle, pair) = backward(
            place,
            doc_len_bwd,
            query_bwd,
            out_grad,
            (own_bwd, middle_bwd, pair_bwd),
            starts[chunk],
            grad_query,
        )
        if chunk > 0:
            pair, parts[-1], query_moved = after(pair, parts[-1], query_moved)
        pair = from_behind(pair, "ctx", -1, f"part_pair_{chunk}")
        middle = (middle.astype(jnp.float32) + pair[1:].astype(jnp.float32)).astype(jnp.bfloat16)
        parts += [own, pair, from_behind(middle, "ctx", -2, f"part_middle_{chunk}")]
    next_stream = forward(place, len_moved, query_moved, (own_fwd, middle_fwd, pair_fwd))
    next_stream, *parts = after(next_stream, *parts)
    grad_key, grad_value = add_parts(parts)
    return (next_stream, grad_query, grad_key, grad_value)


def solution(mesh):
    spec = P("section", "ctx", None)
    row = P("section", None)
    return jax.shard_map(
        on_device,
        mesh=mesh,
        in_specs=(spec, spec, spec, row, spec, spec, spec, row, spec),
        out_specs=(spec, spec, spec, spec),
        check_vma=False,
    )
```

time: 191 us -> 78.5 us (0.41)
  the two profiles are of different devices: /device:TPU:183 before, /device:TPU:30 now
where the time goes in v1:
time: 78.5 us; the launch traced here: 78.4 us
  waiting for transfers between devices  32.6 us (42%)
  Pallas kernels  24.3 us (31%)
  starting transfers between devices  17.3 us (22%)
  local copies, waits for them, and re-layouts  2.39 us (3%)
  other arithmetic  1.06 us (1%)
    ppermute x13, waiting for transfers between devices, from_behind(): lax.ppermute(value, axis, [(at, (at + steps) % count) for at in range(cou...  32.6 us
    ppermute x13, starting transfers between devices, from_behind(): lax.ppermute(value, axis, [(at, (at + steps) % count) for at in range(cou...  17.3 us
    pallas_call x2, Pallas kernels, backward(): pl.pallas_call(backward_kernel, grid=(groups,), out_shape=[jax.ShapeDtype...  14 us
    pallas_call x1, Pallas kernels, forward(): pl.pallas_call(forward_kernel, grid=(KV_HEADS,), out_shape=jax.ShapeDtype...  9.44 us
    slice x1, local copies, waits for them, and re-layouts, on_device(): grad_held[:, :, at * GROUP_WIDTH:to * GROUP_WIDTH]  2.33 us
  transfers between devices with their start and end apart: 13, of which 6 were waited for; matrix products, arithmetic and copies ran while one was open for 1% of the time, Pallas kernels for 30%

profile of v1, /device:TPU:30, one launch (start us, length us, event | category | flops | bytes accessed | tf_op | source)
XLA Modules:
  0.0 78.4 jit_solution(1423329189828573958)
XLA Ops:
  0.6 0.0 copy-start.2
  0.6 0.0 copy-start.3
  0.7 0.0 copy-start.4
  0.7 0.0 copy-start.5
  0.7 2.3 %fusion = (bf16[1,128,2048]{2,1,0:T(8,128)(2,1)}, bf16[1,128,2048]{2,1,0:T(8,128)(2,1)}) fusion(bf16[1,128,4096]{2,1,0:T(8,128)(2,1)} %param.17), kind=kLoop, calls=%fused_computation.8 | loop fusion | bytes 2097152 | tf_op jit(solution)/shard_map/slice | solution.py:246
  3.0 0.0 copy-done.2
  3.0 0.0 copy-start
  3.0 0.0 copy-done.3
  3.1 2.0 %collective-permute-start.4 = (bf16[1,128,1024]{2,1,0:T(8,128)(2,1)S(1)}, bf16[1,128,1024]{2,1,0:T(8,128)(2,1)S(1)}, u32[]{:S(2)}, u32[]{:S(2)}) collective-permute-start(bf16[1,128,1024]{2,1,0:T(8,128)(2,1)S(1)} %constant_dynamic-update-slice_fusion.refs_3_.refs_7_), channel_id=1, source_target_pairs={{0,2},{1,3},{2,4},{3,5},{4,6},{5,7},{6,8},{7,9},{8,10},{9,11},{10,... | collective-permute-start | bytes 786440 | tf_op jit(solution)/shard_map/kv_bwd_middle/ppermute | solution.py:31
  5.0 0.0 copy-done.4
  5.1 0.0 copy-done.5
  5.1 0.0 copy-start.6
  5.1 0.2 collective-permute-start
  5.3 10.0 %collective-permute-done.4.refs_1_.refs_5_ = bf16[1,128,1024]{2,1,0:T(8,128)(2,1)S(1)} collective-permute-done((bf16[1,128,1024]{2,1,0:T(8,128)(2,1)S(1)}, bf16[1,128,1024]{2,1,0:T(8,128)(2,1)S(1)}, u32[]{:S(2)}, u32[]{:S(2)}) %collective-permute-start.4) | collective-permute-done | bytes 262176 | tf_op jit(solution)/shard_map/kv_bwd_middle/ppermute | solution.py:31
  15.3 0.8 %pad_maximum_fusion = bf16[2,128,1024]{2,1,0:T(8,128)(2,1)} fusion(bf16[1,128,1024]{2,1,0:T(8,128)(2,1)S(1)} %collective-permute-done.4.refs_1_.refs_5_, bf16[1,128,1024]{2,1,0:T(8,128)(2,1)S(1)} %constant_dynamic-update-slice_fusion.refs_3_.refs_7_), kind=kLoop, calls=%fused_computation | loop fusion | flops 262144 | bytes 1048576 | tf_op jit(solution)/shard_map/concatenate | solution.py:263
  16.1 0.0 collective-permute-start.5
  16.1 0.8 %collective-permute-start.6 = (bf16[1,128,2048]{2,1,0:T(8,128)(2,1)}, bf16[1,128,2048]{2,1,0:T(8,128)(2,1)}, u32[]{:S(2)}, u32[]{:S(2)}) collective-permute-start(bf16[1,128,2048]{2,1,0:T(8,128)(2,1)} %get-tuple-element.37), channel_id=1, source_target_pairs={{0,240},{16,0},{32,16},{48,32},{64,48},{80,64},{96,80},{112,96},{1... | collective-permute-start | bytes 1572872 | tf_op jit(solution)/shard_map/grad_0/ppermute | solution.py:31
  17.0 0.0 copy-done.6
  17.0 4.5 %collective-permute-start.1 = (s32[1,16]{1,0:T(1,128)S(1)}, s32[1,16]{1,0:T(1,128)S(1)}, u32[]{:S(2)}, u32[]{:S(2)}) collective-permute-start(s32[1,16]{1,0:T(1,128)S(1)} %copy-done.6), channel_id=1, source_target_pairs={{0,16},{16,32},{32,48},{48,64},{64,80},{80,96},{96,112},{112,128},... | collective-permute-start | bytes 200 | tf_op jit(solution)/shard_map/len_moved/ppermute | solution.py:31
  21.5 1.3 %collective-permute-done.1.len_ref = s32[1,16]{1,0:T(1,128)S(1)} collective-permute-done((s32[1,16]{1,0:T(1,128)S(1)}, s32[1,16]{1,0:T(1,128)S(1)}, u32[]{:S(2)}, u32[]{:S(2)}) %collective-permute-start.1) | collective-permute-done | bytes 96 | tf_op jit(solution)/shard_map/len_moved/ppermute | solution.py:31
  22.8 0.0 collective-permute-done.refs_3_.refs_7_
  22.8 5.6 %collective-permute-start.9 = (bf16[1,128,4096]{2,1,0:T(8,128)(2,1)}, bf16[1,128,4096]{2,1,0:T(8,128)(2,1)}, u32[]{:S(2)}, u32[]{:S(2)}) collective-permute-start(bf16[1,128,4096]{2,1,0:T(8,128)(2,1)} %param.9), channel_id=1, source_target_pairs={{0,16},{16,32},{32,48},{48,64},{64,80},{80,96},{96,112},{112,128},... | collective-permute-start | bytes 3145736 | tf_op jit(solution)/shard_map/query_moved/ppermute | solution.py:31
  28.4 0.0 collective-permute-start.3
  28.4 0.0 collective-permute-start.2
  28.4 0.0 copy-start.1
  28.4 0.1 pad_add_fusion.place_ref
  28.4 8.0 %collective-permute-done.3.refs_1_.refs_5_ = bf16[1,128,1024]{2,1,0:T(8,128)(2,1)S(1)} collective-permute-done((bf16[1,128,1024]{2,1,0:T(8,128)(2,1)S(1)}, bf16[1,128,1024]{2,1,0:T(8,128)(2,1)S(1)}, u32[]{:S(2)}, u32[]{:S(2)}) %collective-permute-start.3) | collective-permute-done | bytes 262176 | tf_op jit(solution)/shard_map/kv_fwd_middle/ppermute | solution.py:31
  36.5 0.0 collective-permute-done.5.refs_0_.refs_2_.refs_4_.refs_6_
  36.5 0.0 collective-permute-done.6.grad_ref
  36.5 0.0 copy-done
  36.5 0.0 copy-done.1
  36.5 7.2 %shard_map.120 = (bf16[1,128,4096]{2,1,0:T(8,128)(2,1)}, bf16[1,128,512]{2,1,0:T(8,128)(2,1)S(1)}, bf16[1,128,512]{2,1,0:T(8,128)(2,1)S(1)}, bf16[2,128,512]{2,1,0:T(8,128)(2,1)S(1)}) custom-call(s32[3]{0:T(128)S(1)} %pad_add_fusion.place_ref, s32[1,16]{1,0:T(1,128)S(1)} %copy-done.1, bf16[1,128,4096]{2,1,0:T(8,128)(2,1)S(1)} %copy-done, ...), custom_call_target="tpu_custom_call" | custom-call | flops 1342177280 | bytes 2097152 | tf_op jit(solution)/shard_map/pallas_call | solution.py:184
  43.7 0.5 collective-permute-start.7
  44.2 3.9 %collective-permute-done.7.refs_1_ = bf16[2,128,512]{2,1,0:T(8,128)(2,1)S(1)} collective-permute-done((bf16[2,128,512]{2,1,0:T(8,128)(2,1)S(1)}, bf16[2,128,512]{2,1,0:T(8,128)(2,1)S(1)}, u32[]{:S(2)}, u32[]{:S(2)}) %collective-permute-start.7) | collective-permute-done | bytes 262176 | tf_op jit(solution)/shard_map/part_pair_0/ppermute | solution.py:31
  48.1 1.3 %collective-permute-start.8 = (bf16[1,128,512]{2,1,0:T(8,128)(2,1)S(1)}, bf16[1,128,512]{2,1,0:T(8,128)(2,1)S(1)}, u32[]{:S(2)}, u32[]{:S(2)}) collective-permute-start(bf16[1,128,512]{2,1,0:T(8,128)(2,1)S(1)} %add_convert_fusion.1), channel_id=1, source_target_pairs={{0,14},{1,15},{2,0},{3,1},{4,2},{5,3},{6,4},{7,5},{8,6},{9,7},{10,... | collective-permute-start | bytes 393224 | tf_op jit(solution)/shard_map/part_middle_0/ppermute | solution.py:31
  49.4 0.0 collective-permute-done.2.grad_ref
  49.4 6.9 %shard_map.121 = (bf16[1,128,4096]{2,1,0:T(8,128)(2,1)}, bf16[1,128,512]{2,1,0:T(8,128)(2,1)S(1)}, bf16[1,128,512]{2,1,0:T(8,128)(2,1)S(1)}, bf16[2,128,512]{2,1,0:T(8,128)(2,1)S(1)}) custom-call(s32[3]{0:T(128)S(1)} %pad_add_fusion.place_ref, s32[1,16]{1,0:T(1,128)S(1)} %copy-done.1, ...), custom_call_target="tpu_custom_call", output_to_operand_aliasing={{0}: (12, {})} | custom-call | flops 1342177280 | bytes 2097152 | tf_op jit(solution)/shard_map/pallas_call | solution.py:184
  56.3 0.0 collective-permute-done.8.refs_2_
  56.3 0.0 collective-permute-done.9.query_ref
  56.3 1.9 %collective-permute-start.11 = (bf16[2,128,512]{2,1,0:T(8,128)(2,1)S(1)}, bf16[2,128,512]{2,1,0:T(8,128)(2,1)S(1)}, u32[]{:S(2)}, u32[]{:S(2)}) collective-permute-start(bf16[2,128,512]{2,1,0:T(8,128)(2,1)S(1)} %get-tuple-element.48), channel_id=1, source_target_pairs={{0,15},{1,0},{2,1},{3,2},{4,3},{5,4},{6,5},{7,6},{8,7},{9,8},{10,9... | collective-permute-start | bytes 786440 | tf_op jit(solution)/shard_map/part_pair_1/ppermute | solution.py:31
  58.2 0.1 pad_maximum_fusion.1
  58.3 0.1 collective-permute-start.10
  58.4 3.8 %collective-permute-done.11.refs_4_ = bf16[2,128,512]{2,1,0:T(8,128)(2,1)S(1)} collective-permute-done((bf16[2,128,512]{2,1,0:T(8,128)(2,1)S(1)}, bf16[2,128,512]{2,1,0:T(8,128)(2,1)S(1)}, u32[]{:S(2)}, u32[]{:S(2)}) %collective-permute-start.11) | collective-permute-done | bytes 262176 | tf_op jit(solution)/shard_map/part_pair_1/ppermute | solution.py:31
  62.2 0.3 collective-permute-start.12
  62.5 5.6 %collective-permute-done.10.refs_0_.refs_2_.refs_4_.refs_6_ = bf16[2,128,1024]{2,1,0:T(8,128)(2,1)S(1)} collective-permute-done((bf16[2,128,1024]{2,1,0:T(8,128)(2,1)S(1)}, bf16[2,128,1024]{2,1,0:T(8,128)(2,1)S(1)}, u32[]{:S(2)}, u32[]{:S(2)}) %collective-permute-start.10) | collective-permute-done | bytes 524320 | tf_op jit(solution)/shard_map/kv_fwd_pair/ppermute | solution.py:31
  68.1 9.4 %shard_map.122 = bf16[1,128,4096]{2,1,0:T(8,128)(2,1)} custom-call(s32[3]{0:T(128)S(1)} %pad_add_fusion.place_ref, s32[1,16]{1,0:T(1,128)S(1)} %collective-permute-done.1.len_ref, bf16[1,128,4096]{2,1,0:T(8,128)(2,1)} %collective-permute-done.9.query_ref, bf16[2,128,1024]{2,1,0:T(8,128)(2,1)S(1)} %collective-permute-done.10.refs_0_.refs_2_.refs_4_.refs_6_, ...), custom_call_target="tpu_custom_call" | custom-call | flops 1073741824 | bytes 3145728 | tf_op jit(solution)/shard_map/pallas_call | solution.py:160
  77.6 0.0 collective-permute-done.12.refs_5_
  77.6 0.8 %shard_map.123 = (bf16[1,128,512]{2,1,0:T(8,128)(2,1)}, bf16[1,128,512]{2,1,0:T(8,128)(2,1)}) custom-call(bf16[1,128,512]{2,1,0:T(8,128)(2,1)S(1)} %get-tuple-element.52.refs_0_, bf16[2,128,512]{2,1,0:T(8,128)(2,1)S(1)} %collective-permute-done.7.refs_1_, bf16[1,128,512]{2,1,0:T(8,128)(2,1)S(1)} %collective-permute-done.8.refs_2_, ...), custom_call_target="tpu_custom_call" | custom-call | bytes 2097152 | tf_op jit(solution)/shard_map/pallas_call | solution.py:217
  (5 shorter events, 0.1 us)
Async XLA Ops:
  0.6 2.4 %copy-start.2 = (bf16[1,128,512]{2,1,0:T(8,128)(2,1)S(1)}, bf16[1,128,512]{2,1,0:T(8,128)(2,1)}, u32[]{:S(2)}) copy-start(bf16[1,128,512]{2,1,0:T(8,128)(2,1)} %param.14) | copy-start | bytes 393220
  0.6 2.4 %copy-start.3 = (bf16[1,128,512]{2,1,0:T(8,128)(2,1)S(1)}, bf16[1,128,512]{2,1,0:T(8,128)(2,1)}, u32[]{:S(2)}) copy-start(bf16[1,128,512]{2,1,0:T(8,128)(2,1)} %param.15) | copy-start | bytes 393220
  0.7 4.4 %copy-start.4 = (bf16[1,128,512]{2,1,0:T(8,128)(2,1)S(1)}, bf16[1,128,512]{2,1,0:T(8,128)(2,1)}, u32[]{:S(2)}) copy-start(bf16[1,128,512]{2,1,0:T(8,128)(2,1)} %param.11) | copy-start | bytes 393220
  0.7 4.4 %copy-start.5 = (bf16[1,128,512]{2,1,0:T(8,128)(2,1)S(1)}, bf16[1,128,512]{2,1,0:T(8,128)(2,1)}, u32[]{:S(2)}) copy-start(bf16[1,128,512]{2,1,0:T(8,128)(2,1)} %param.10) | copy-start | bytes 393220
  3.0 33.5 %copy-start = (bf16[1,128,4096]{2,1,0:T(8,128)(2,1)S(1)}, bf16[1,128,4096]{2,1,0:T(8,128)(2,1)}, u32[]{:S(2)}) copy-start(bf16[1,128,4096]{2,1,0:T(8,128)(2,1)} %query_ref.3) | copy-start | bytes 3145732
  3.1 12.2 %collective-permute-start.4 = (bf16[1,128,1024]{2,1,0:T(8,128)(2,1)S(1)}, bf16[1,128,1024]{2,1,0:T(8,128)(2,1)S(1)}, u32[]{:S(2)}, u32[]{:S(2)}) collective-permute-start(bf16[1,128,1024]{2,1,0:T(8,128)(2,1)S(1)} %constant_dynamic-update-slice_fusion.refs_3_.refs_7_), channel_id=1, source_target_pairs={{0,2},{1,3},{2,4},{3,5},{4,6},{5,7},{6,8},{7,9},{8,10},{9,11},{10,... | collective-permute-start | bytes 786440 | tf_op jit(solution)/shard_map/kv_bwd_middle/ppermute | solution.py:31
  5.1 11.9 %copy-start.6 = (s32[1,16]{1,0:T(1,128)S(1)}, s32[1,16]{1,0:T(1,128)}, u32[]{:S(2)}) copy-start(s32[1,16]{1,0:T(1,128)} %param.12) | copy-start | bytes 196
  5.1 17.7 %collective-permute-start = (bf16[1,128,1024]{2,1,0:T(8,128)(2,1)S(1)}, bf16[1,128,1024]{2,1,0:T(8,128)(2,1)S(1)}, u32[]{:S(2)}, u32[]{:S(2)}) collective-permute-start(bf16[1,128,1024]{2,1,0:T(8,128)(2,1)S(1)} %pad_maximum_fusion.2), channel_id=1, source_target_pairs={{0,16},{16,32},{32,48},{48,64},{64,80},{80,96},{96,112},{112,128},... | collective-permute-start | bytes 786440 | tf_op jit(solution)/shard_map/kv_moved/ppermute | solution.py:31
  16.1 20.3 %collective-permute-start.5 = (bf16[2,128,1024]{2,1,0:T(8,128)(2,1)}, bf16[2,128,1024]{2,1,0:T(8,128)(2,1)S(1)}, u32[]{:S(2)}, u32[]{:S(2)}) collective-permute-start(bf16[2,128,1024]{2,1,0:T(8,128)(2,1)} %pad_maximum_fusion), channel_id=1, source_target_pairs={{0,1},{1,2},{2,3},{3,4},{4,5},{5,6},{6,7},{7,8},{8,9},{9,10},{10,1... | collective-permute-start | bytes 1572872 | tf_op jit(solution)/shard_map/kv_bwd_pair/ppermute | solution.py:31
  16.1 20.3 %collective-permute-start.6 = (bf16[1,128,2048]{2,1,0:T(8,128)(2,1)}, bf16[1,128,2048]{2,1,0:T(8,128)(2,1)}, u32[]{:S(2)}, u32[]{:S(2)}) collective-permute-start(bf16[1,128,2048]{2,1,0:T(8,128)(2,1)} %get-tuple-element.37), channel_id=1, source_target_pairs={{0,240},{16,0},{32,16},{48,32},{64,48},{80,64},{96,80},{112,96},{1... | collective-permute-start | bytes 1572872 | tf_op jit(solution)/shard_map/grad_0/ppermute | solution.py:31
  17.0 5.8 %collective-permute-start.1 = (s32[1,16]{1,0:T(1,128)S(1)}, s32[1,16]{1,0:T(1,128)S(1)}, u32[]{:S(2)}, u32[]{:S(2)}) collective-permute-start(s32[1,16]{1,0:T(1,128)S(1)} %copy-done.6), channel_id=1, source_target_pairs={{0,16},{16,32},{32,48},{48,64},{64,80},{80,96},{96,112},{112,128},... | collective-permute-start | bytes 200 | tf_op jit(solution)/shard_map/len_moved/ppermute | solution.py:31
  22.8 33.5 %collective-permute-start.9 = (bf16[1,128,4096]{2,1,0:T(8,128)(2,1)}, bf16[1,128,4096]{2,1,0:T(8,128)(2,1)}, u32[]{:S(2)}, u32[]{:S(2)}) collective-permute-start(bf16[1,128,4096]{2,1,0:T(8,128)(2,1)} %param.9), channel_id=1, source_target_pairs={{0,16},{16,32},{32,48},{48,64},{64,80},{80,96},{96,112},{112,128},... | collective-permute-start | bytes 3145736 | tf_op jit(solution)/shard_map/query_moved/ppermute | solution.py:31
  28.4 8.1 %collective-permute-start.3 = (bf16[1,128,1024]{2,1,0:T(8,128)(2,1)S(1)}, bf16[1,128,1024]{2,1,0:T(8,128)(2,1)S(1)}, u32[]{:S(2)}, u32[]{:S(2)}) collective-permute-start(bf16[1,128,1024]{2,1,0:T(8,128)(2,1)S(1)} %collective-permute-done.refs_3_.refs_7_), channel_id=1, source_target_pairs={{0,2},{1,3},{2,4},{3,5},{4,6},{5,7},{6,8},{7,9},{8,10},{9,11},{10,... | collective-permute-start | bytes 786440 | tf_op jit(solution)/shard_map/kv_fwd_middle/ppermute | solution.py:31
  28.4 21.1 %collective-permute-start.2 = (bf16[1,128,2048]{2,1,0:T(8,128)(2,1)}, bf16[1,128,2048]{2,1,0:T(8,128)(2,1)S(1)}, u32[]{:S(2)}, u32[]{:S(2)}) collective-permute-start(bf16[1,128,2048]{2,1,0:T(8,128)(2,1)} %get-tuple-element.60), channel_id=1, source_target_pairs={{0,240},{16,0},{32,16},{48,32},{64,48},{80,64},{96,80},{112,96},{1... | collective-permute-start | bytes 1572872 | tf_op jit(solution)/shard_map/grad_1/ppermute | solution.py:31
  28.4 8.1 %copy-start.1 = (s32[1,16]{1,0:T(1,128)S(1)}, s32[1,16]{1,0:T(1,128)}, u32[]{:S(2)}) copy-start(s32[1,16]{1,0:T(1,128)} %len_ref.3) | copy-start | bytes 196
  43.7 4.4 %collective-permute-start.7 = (bf16[2,128,512]{2,1,0:T(8,128)(2,1)S(1)}, bf16[2,128,512]{2,1,0:T(8,128)(2,1)S(1)}, u32[]{:S(2)}, u32[]{:S(2)}) collective-permute-start(bf16[2,128,512]{2,1,0:T(8,128)(2,1)S(1)} %get-tuple-element.41), channel_id=1, source_target_pairs={{0,15},{1,0},{2,1},{3,2},{4,3},{5,4},{6,5},{7,6},{8,7},{9,8},{10,9... | collective-permute-start | bytes 786440 | tf_op jit(solution)/shard_map/part_pair_0/ppermute | solution.py:31
  48.1 8.2 %collective-permute-start.8 = (bf16[1,128,512]{2,1,0:T(8,128)(2,1)S(1)}, bf16[1,128,512]{2,1,0:T(8,128)(2,1)S(1)}, u32[]{:S(2)}, u32[]{:S(2)}) collective-permute-start(bf16[1,128,512]{2,1,0:T(8,128)(2,1)S(1)} %add_convert_fusion.1), channel_id=1, source_target_pairs={{0,14},{1,15},{2,0},{3,1},{4,2},{5,3},{6,4},{7,5},{8,6},{9,7},{10,... | collective-permute-start | bytes 393224 | tf_op jit(solution)/shard_map/part_middle_0/ppermute | solution.py:31
  56.3 5.8 %collective-permute-start.11 = (bf16[2,128,512]{2,1,0:T(8,128)(2,1)S(1)}, bf16[2,128,512]{2,1,0:T(8,128)(2,1)S(1)}, u32[]{:S(2)}, u32[]{:S(2)}) collective-permute-start(bf16[2,128,512]{2,1,0:T(8,128)(2,1)S(1)} %get-tuple-element.48), channel_id=1, source_target_pairs={{0,15},{1,0},{2,1},{3,2},{4,3},{5,4},{6,5},{7,6},{8,7},{9,8},{10,9... | collective-permute-start | bytes 786440 | tf_op jit(solution)/shard_map/part_pair_1/ppermute | solution.py:31
  58.3 9.8 %collective-permute-start.10 = (bf16[2,128,1024]{2,1,0:T(8,128)(2,1)S(1)}, bf16[2,128,1024]{2,1,0:T(8,128)(2,1)S(1)}, u32[]{:S(2)}, u32[]{:S(2)}) collective-permute-start(bf16[2,128,1024]{2,1,0:T(8,128)(2,1)S(1)} %pad_maximum_fusion.1), channel_id=1, source_target_pairs={{0,1},{1,2},{2,3},{3,4},{4,5},{5,6},{6,7},{7,8},{8,9},{9,10},{10,1... | collective-permute-start | bytes 1572872 | tf_op jit(solution)/shard_map/kv_fwd_pair/ppermute | solution.py:31
  62.2 15.4 %collective-permute-start.12 = (bf16[1,128,512]{2,1,0:T(8,128)(2,1)S(1)}, bf16[1,128,512]{2,1,0:T(8,128)(2,1)S(1)}, u32[]{:S(2)}, u32[]{:S(2)}) collective-permute-start(bf16[1,128,512]{2,1,0:T(8,128)(2,1)S(1)} %add_convert_fusion), channel_id=1, source_target_pairs={{0,14},{1,15},{2,0},{3,1},{4,2},{5,3},{6,4},{7,5},{8,6},{9,7},{10,... | collective-permute-start | bytes 393224 | tf_op jit(solution)/shard_map/part_middle_1/ppermute | solution.py:31

commit v2 on v1

v2 whole, which is shorter than its diff:
```python
import math

import jax
import jax.numpy as jnp
from jax import lax
from jax.experimental import pallas as pl
from jax.experimental.pallas import tpu as pltpu
from jax.sharding import PartitionSpec as P

HEADS = 32
KV_HEADS = 4
GROUP = HEADS // KV_HEADS
HEAD_DIM = 128
REACH = 3
ROWS = 128
KEYS = (REACH + 1) * ROWS
DOCS = 16
SCALE = HEAD_DIM**-0.5
SCALE_LOG2 = SCALE * math.log2(math.e)
MASKED = -1e30
KV_WIDTH = KV_HEADS * HEAD_DIM
GROUP_WIDTH = GROUP * HEAD_DIM
CHUNKS = (4,)
FOLDS = ((0,),)
HEADS_AT_ONCE = 4
VMEM = 24 * 1024 * 1024
COST = 1
PACK_COST = 1
PACK_VMEM = 56 * 1024 * 1024
SMALL_VMEM = 8 * 1024 * 1024
NT = (((1,), (1,)), ((), ()))


def from_behind(value, axis, steps, what="moved"):
    count = lax.axis_size(axis)
    with jax.named_scope(what):
        return lax.ppermute(value, axis, [(at, (at + steps) % count) for at in range(count)])


def swapped(value, what):
    count = lax.axis_size("ctx")
    with jax.named_scope(what):
        return lax.ppermute(value, "ctx", [(at, at ^ 1) for at in range(count)])


def second_core():
    return lax.rem(lax.axis_index("ctx"), 2) == 1


def after(value, *earlier):
    return lax.optimization_barrier((value, *earlier))[0]


def params(limit):
    return pltpu.CompilerParams(vmem_limit_bytes=limit)


def cost(flops, bytes_accessed):
    return pl.CostEstimate(flops=flops, bytes_accessed=bytes_accessed, transcendentals=0)


def first_keys(len_ref, columns):
    shard = lax.axis_index("ctx")
    query = shard * ROWS + lax.broadcasted_iota(jnp.int32, (ROWS, columns), 0)
    start = jnp.zeros((ROWS, columns), jnp.int32)
    end = jnp.int32(0)
    for doc in range(DOCS):
        end = end + len_ref[0, doc]
        start = jnp.where(query >= end, end, start)
    return start - (shard - REACH) * ROWS


def fill_bias(first, bias_ref):
    query = REACH * ROWS + lax.broadcasted_iota(jnp.int32, (ROWS, ROWS), 0)
    for piece in range(REACH + 1):
        key = piece * ROWS + lax.broadcasted_iota(jnp.int32, (ROWS, ROWS), 1)
        seen = (key >= first) & (key <= query)
        bias_ref[:, piece * ROWS : (piece + 1) * ROWS] = jnp.where(seen, 0.0, MASKED)


def head(index):
    return slice(index * HEAD_DIM, (index + 1) * HEAD_DIM)


def weights_of(queries, keys, bias):
    scores = lax.dot_general(queries, keys, NT, preferred_element_type=jnp.float32) + bias
    top = jnp.max(scores, axis=1, keepdims=True)
    return jnp.exp2((scores - top) * SCALE_LOG2)


def stacked(refs):
    return jnp.concatenate([ref[0] for ref in refs], axis=0)


def stack_heads(ref, first, count):
    return jnp.concatenate([ref[0, :, head(first + index)] for index in range(count)], axis=0)


def forward_kernel(first_ref, query_ref, *refs):
    key_refs, value_refs, (out_ref, bias_ref) = refs[:4], refs[4:8], refs[8:]

    @pl.when(pl.program_id(0) == 0)
    def _():
        high, low = (first_ref[0, :, at : at + 1].astype(jnp.float32) for at in (0, 64))
        fill_bias((high * 256.0 + low).astype(jnp.int32), bias_ref)

    keep = (lax.axis_index("section") > 0).astype(jnp.float32)
    keys = stacked(key_refs)
    values = jnp.concatenate(
        [stacked(value_refs), jnp.ones((KEYS, HEAD_DIM), jnp.bfloat16)], axis=1
    )
    for index in range(GROUP):
        weights = weights_of(query_ref[0, :, head(index)], keys, bias_ref[...])
        mixed = jnp.dot(weights.astype(jnp.bfloat16), values, preferred_element_type=jnp.float32)
        result = mixed[:, :HEAD_DIM] * keep / mixed[:, HEAD_DIM:]
        out_ref[0, :, head(index)] = result.astype(jnp.bfloat16)


def probs_kernel(len_ref, query_ref, *refs):
    key_refs, (out_ref, bias_ref) = refs[:4], refs[4:]

    @pl.when(pl.program_id(0) == 0)
    def _():
        fill_bias(first_keys(len_ref, ROWS), bias_ref)

    keys = stacked(key_refs)
    for first in range(0, GROUP, HEADS_AT_ONCE):
        queries = stack_heads(query_ref, first, HEADS_AT_ONCE)
        weights = weights_of(queries, keys, jnp.concatenate([bias_ref[...]] * HEADS_AT_ONCE, axis=0))
        total = jnp.sum(weights, axis=1, keepdims=True)
        out_ref[0, first * ROWS : (first + HEADS_AT_ONCE) * ROWS, :] = weights * (1.0 / total)


def backward_kernel(probs_ref, query_ref, grad_ref, *refs):
    key_refs, value_refs = refs[:4], refs[4:8]
    (
        out_ref, own_ref, middle_ref, near_ref, far_ref, queries_ref, grads_ref, scores_ref, low_ref
    ) = refs[-9:]
    last = lax.axis_size("section") - 1
    keep = (lax.axis_index("section") < last).astype(jnp.float32).astype(jnp.bfloat16)
    keys, values = stacked(key_refs), stacked(value_refs)
    queries_ref[...] = stack_heads(query_ref, 0, GROUP)
    grads_ref[...] = stack_heads(grad_ref, 0, GROUP) * keep
    for first in range(0, GROUP, HEADS_AT_ONCE):
        at = slice(first * ROWS, (first + HEADS_AT_ONCE) * ROWS)
        probs = probs_ref[0, at, :]
        d_prob = lax.dot_general(grads_ref[at, :], values, NT, preferred_element_type=jnp.float32)
        delta = jnp.sum(probs * d_prob, axis=1, keepdims=True)
        scores_ref[at, :] = (probs * (d_prob - delta)).astype(jnp.bfloat16)
        low_ref[at, :] = probs.astype(jnp.bfloat16)
    d_query = jnp.dot(scores_ref[...], keys, preferred_element_type=jnp.float32) * SCALE
    for index in range(GROUP):
        out_ref[0, :, head(index)] = d_query[index * ROWS : (index + 1) * ROWS].astype(
            jnp.bfloat16
        )
    d_key = jnp.dot(queries_ref[...].T, scores_ref[...], preferred_element_type=jnp.float32).T
    d_value = jnp.dot(grads_ref[...].T, low_ref[...], preferred_element_type=jnp.float32).T
    for piece, part_ref in enumerate((far_ref, middle_ref, near_ref, own_ref)):
        at = slice(piece * ROWS, (piece + 1) * ROWS)
        part_ref[0, :, :HEAD_DIM] = (d_key[at] * SCALE).astype(jnp.bfloat16)
        part_ref[0, :, HEAD_DIM:] = d_value[at].astype(jnp.bfloat16)


def small_call(
    kernel, operands, in_specs, shapes, out_specs, steps, limit=SMALL_VMEM, bytes_accessed=COST
):
    return pl.pallas_call(
        kernel,
        grid=(steps,),
        out_shape=[jax.ShapeDtypeStruct(shape, jnp.bfloat16) for shape in shapes],
        in_specs=in_specs,
        out_specs=out_specs,
        cost_estimate=cost(COST, bytes_accessed),
        compiler_params=params(limit),
    )(*operands)


def row_spec(width, steps, column=0):
    return pl.BlockSpec((1, ROWS // steps, width), lambda i: (0, i, column))


def pack_kernel(len_ref, key_fwd, value_fwd, key_bwd, value_bwd, fwd_ref, bwd_ref):
    for key_ref, value_ref, out_ref in (
        (key_fwd, value_fwd, fwd_ref),
        (key_bwd, value_bwd, bwd_ref),
    ):
        out_ref[0, :, :KV_WIDTH] = key_ref[0]
        out_ref[0, :, KV_WIDTH : 2 * KV_WIDTH] = value_ref[0]
    first = first_keys(len_ref, ROWS)
    high = jnp.where(first >= 256, 1, 0)
    left = lax.broadcasted_iota(jnp.int32, (ROWS, ROWS), 1) < ROWS // 2
    coded = jnp.where(left, high, first - 256 * high)
    fwd_ref[0, :, 2 * KV_WIDTH :] = coded.astype(jnp.float32).astype(jnp.bfloat16)


def pack(lengths, *keys_and_values):
    widths = [2 * KV_WIDTH + ROWS, 2 * KV_WIDTH]
    return small_call(
        pack_kernel,
        (lengths, *keys_and_values),
        [pl.BlockSpec(memory_space=pltpu.SMEM)] + [row_spec(KV_WIDTH, 1)] * 4,
        [(1, ROWS, width) for width in widths],
        [row_spec(width, 1) for width in widths],
        1,
        PACK_VMEM,
        PACK_COST,
    )


def folded(middles, fars, nears):
    sums = []
    for middle, far, near in zip(middles, fars, nears):
        total = middle.astype(jnp.float32) + far.astype(jnp.float32)
        total = total + jnp.where(second_core(), near.astype(jnp.float32), 0.0)
        sums.append(total.astype(jnp.bfloat16))
    return sums[0] if len(sums) == 1 else jnp.concatenate(sums, axis=2)


def group_spec(first):
    return pl.BlockSpec((1, ROWS, GROUP_WIDTH), lambda i: (0, 0, first + i))


def key_specs(first):
    return [pl.BlockSpec((1, ROWS, HEAD_DIM), lambda i: (0, 0, first + i))] * 4


def value_specs(first):
    return key_specs(KV_HEADS + first)


def forward(query, pieces):
    return pl.pallas_call(
        forward_kernel,
        grid=(KV_HEADS,),
        out_shape=jax.ShapeDtypeStruct(query.shape, jnp.bfloat16),
        in_specs=[
            pl.BlockSpec((1, ROWS, ROWS), lambda i: (0, 0, 2 * KV_HEADS)),
            group_spec(0),
        ]
        + key_specs(0)
        + value_specs(0),
        out_specs=group_spec(0),
        scratch_shapes=[pltpu.VMEM((ROWS, KEYS), jnp.float32)],
        cost_estimate=cost(COST, COST),
        compiler_params=params(VMEM),
    )(pieces[-1], query, *pieces, *pieces)


def probabilities(lengths, query, pieces):
    block = (1, GROUP * ROWS, KEYS)
    return pl.pallas_call(
        probs_kernel,
        grid=(KV_HEADS,),
        out_shape=jax.ShapeDtypeStruct((KV_HEADS,) + block[1:], jnp.float32),
        in_specs=[pl.BlockSpec(memory_space=pltpu.SMEM), group_spec(0)] + key_specs(0),
        out_specs=pl.BlockSpec(block, lambda i: (i, 0, 0)),
        scratch_shapes=[pltpu.VMEM((ROWS, KEYS), jnp.float32)],
        cost_estimate=cost(COST, COST),
        compiler_params=params(VMEM),
    )(lengths, query, *pieces)


def backward(probs, query, out_grad, pieces, first, groups, so_far):
    width = groups * 2 * HEAD_DIM
    in_specs = [pl.BlockSpec((1, GROUP * ROWS, KEYS), lambda i: (first + i, 0, 0))]
    in_specs += [group_spec(first)] * 2 + key_specs(first) + value_specs(first)
    operands = [probs, query, out_grad, *pieces, *pieces]
    aliases = {}
    if so_far is not None:
        in_specs.append(pl.BlockSpec(memory_space=pl.ANY))
        aliases = {len(operands): 0}
        operands.append(so_far)
    result = pl.pallas_call(
        backward_kernel,
        grid=(groups,),
        out_shape=[jax.ShapeDtypeStruct(query.shape, jnp.bfloat16)]
        + [jax.ShapeDtypeStruct((1, ROWS, width), jnp.bfloat16)] * 4,
        in_specs=in_specs,
        out_specs=[group_spec(first)]
        + [pl.BlockSpec((1, ROWS, 2 * HEAD_DIM), lambda i: (0, 0, i))] * 4,
        scratch_shapes=[
            pltpu.VMEM((GROUP * ROWS, HEAD_DIM), jnp.bfloat16),
            pltpu.VMEM((GROUP * ROWS, HEAD_DIM), jnp.bfloat16),
            pltpu.VMEM((GROUP * ROWS, KEYS), jnp.bfloat16),
            pltpu.VMEM((GROUP * ROWS, KEYS), jnp.bfloat16),
        ],
        input_output_aliases=aliases,
        cost_estimate=cost(COST, COST),
        compiler_params=params(VMEM),
    )(*operands)
    return result[0], result[1:]


def add_kernel(*refs):
    chunks = len(CHUNKS)
    own_refs, near_refs, fold_refs = refs[:chunks], refs[chunks : 2 * chunks], refs[2 * chunks : -2]
    key_ref, value_ref = refs[-2:]
    folds = [
        (ref, at)
        for ref, members in zip(fold_refs, FOLDS)
        for at in [sum(CHUNKS[chunk] for chunk in members[:spot]) for spot in range(len(members))]
    ]
    first = 0
    first_core = lax.rem(lax.axis_index("ctx"), 2) == 0
    for groups, own_ref, near_ref, (fold_ref, at) in zip(CHUNKS, own_refs, near_refs, folds):
        for group in range(groups):
            here = slice(2 * group * HEAD_DIM, 2 * (group + 1) * HEAD_DIM)
            there = slice(2 * (at + group) * HEAD_DIM, 2 * (at + group + 1) * HEAD_DIM)
            total = own_ref[0, :, here].astype(jnp.float32)
            near = near_ref[0, :, here].astype(jnp.float32)
            total = total + jnp.where(first_core, near, 0.0)
            total = (total + fold_ref[0, :, there].astype(jnp.float32)).astype(jnp.bfloat16)
            key_ref[0, :, head(first + group)] = total[:, :HEAD_DIM]
            value_ref[0, :, head(first + group)] = total[:, HEAD_DIM:]
        first += groups


def add_parts(*parts):
    return small_call(
        add_kernel,
        parts,
        [row_spec(part.shape[2], 1) for part in parts],
        [(1, ROWS, KV_WIDTH)] * 2,
        [row_spec(KV_WIDTH, 1)] * 2,
        1,
    )


def gather_behind(own, what, *earlier):
    middle = from_behind(after(own, *earlier), "ctx", 2, what + "_middle")
    far = from_behind(middle, "ctx", 1, what + "_far")
    near = swapped(jnp.where(second_core(), middle, own), what + "_near")
    return far, middle, near, own


def on_device(
    query_fwd,
    key_fwd,
    value_fwd,
    doc_len_fwd,
    query_bwd,
    key_bwd,
    value_bwd,
    doc_len_bwd,
    grad_held,
):
    out_grad = from_behind(grad_held, "section", -1, "grad")
    kv_fwd, own_bwd = pack(doc_len_fwd, key_fwd, value_fwd, key_bwd, value_bwd)
    own_fwd = from_behind(kv_fwd, "section", 1, "kv_moved")
    pieces_bwd = gather_behind(own_bwd, "kv_bwd", kv_fwd)
    query_moved = from_behind(after(query_fwd, own_fwd), "section", 1, "query_moved")
    probs = probabilities(doc_len_bwd, query_bwd, pieces_bwd)
    pieces_fwd = gather_behind(own_fwd, "kv_fwd", probs)
    grad_query = None
    first = 0
    owns, middles, nears, fars, folds = [], [], [], [], []
    for chunk, groups in enumerate(CHUNKS):
        grad_query, (own, middle, near, far) = backward(
            probs, query_bwd, out_grad, pieces_bwd, first, groups, grad_query
        )
        first += groups
        if chunk > 0:
            far = after(far, fars[0])
        owns.append(own)
        middles.append(middle)
        fars.append(from_behind(far, "ctx", -1, f"part_far_{chunk}"))
        nears.append(swapped(near, f"part_near_{chunk}"))
    for members in FOLDS:
        fold = folded(*([values[chunk] for chunk in members] for values in (middles, fars, nears)))
        if members == FOLDS[-1]:
            fold = after(fold, query_moved)
        folds.append(from_behind(fold, "ctx", -2, f"part_fold_{members[0]}"))
    next_stream = forward(query_moved, pieces_fwd)
    grad_key, grad_value = add_parts(after(owns[0], next_stream), *owns[1:], *nears, *folds)
    return (next_stream, grad_query, grad_key, grad_value)


def solution(mesh):
    spec = P("section", "ctx", None)
    row = P("section", None)
    return jax.shard_map(
        on_device,
        mesh=mesh,
        in_specs=(spec, spec, spec, row, spec, spec, spec, row, spec),
        out_specs=(spec, spec, spec, spec),
        check_vma=False,
    )
```

time: 78.5 us -> 58.3 us (0.74)
  the two profiles are of different devices: /device:TPU:30 before, /device:TPU:96 now
where the time goes in v2:
time: 58.3 us; the launch traced here: 58.1 us
  waiting for transfers between devices  23.9 us (41%)
  Pallas kernels  18.4 us (32%)
  starting transfers between devices  11.1 us (19%)
  local copies, waits for them, and re-layouts  2.83 us (5%)
  other arithmetic  1.14 us (2%)
  between operations  0.71 us (1%)
    ppermute x9, waiting for transfers between devices, from_behind(): lax.ppermute(value, axis, [(at, (at + steps) % count) for at in range(cou...  23.9 us
    ppermute x9, starting transfers between devices, from_behind(): lax.ppermute(value, axis, [(at, (at + steps) % count) for at in range(cou...  10.4 us
    pallas_call x1, Pallas kernels, backward(): pl.pallas_call(backward_kernel, grid=(groups,), out_shape=[jax.ShapeDtype...  6.25 us
    pallas_call x1, Pallas kernels, forward(): pl.pallas_call(forward_kernel, grid=(KV_HEADS,), out_shape=jax.ShapeDtype...  5.16 us
    pallas_call x1, Pallas kernels, probabilities(): pl.pallas_call(probs_kernel, grid=(KV_HEADS,), out_shape=jax.ShapeDtypeSt...  4.15 us
    pallas_call x2, Pallas kernels, small_call(): pl.pallas_call(kernel, grid=(steps,), out_shape=[jax.ShapeDtypeStruct(sha...  2.85 us
    unnamed x8, local copies, waits for them, and re-layouts  2.83 us
  transfers between devices with their start and end apart: 12, of which 6 were waited for; matrix products, arithmetic and copies ran while one was open for 2% of the time, Pallas kernels for 27%

profile of v2, /device:TPU:96, one launch (start us, length us, event | category | flops | bytes accessed | tf_op | source)
XLA Modules:
  0.0 58.1 jit_solution(14354062862749828926)
XLA Ops:
  0.6 0.0 copy-start.1
  0.6 2.0 %shard_map.120 = (bf16[1,128,1152]{2,1,0:T(8,128)(2,1)}, bf16[1,128,1024]{2,1,0:T(8,128)(2,1)}) custom-call(s32[1,16]{1,0:T(1,128)} %len_ref.2, bf16[1,128,512]{2,1,0:T(8,128)(2,1)} %key_fwd.1, bf16[1,128,512]{2,1,0:T(8,128)(2,1)} %value_fwd.1, bf16[1,128,512]{2,1,0:T(8,128)(2,1)} %key_bwd.1, bf16[1,128,512]{2,1,0:T(8,128)(2,1)} %value_bwd.1), custom_call_target="tpu_custom_call" | custom-call | flops 1 | bytes 1 | tf_op jit(solution)/shard_map/pallas_call | solution.py:167
  2.7 3.1 %collective-permute-start.2 = (bf16[1,128,1024]{2,1,0:T(8,128)(2,1)}, bf16[1,128,1024]{2,1,0:T(8,128)(2,1)S(1)}, u32[]{:S(2)}, u32[]{:S(2)}) collective-permute-start(bf16[1,128,1024]{2,1,0:T(8,128)(2,1)} %get-tuple-element.21.refs_3_.refs_7_), channel_id=1, source_target_pairs={{0,2},{1,3},{2,4},{3,5},{4,6},{5,7},{6,8},{7,9},{8,10},{9,11},{10,... | collective-permute-start | bytes 786440 | tf_op jit(solution)/shard_map/kv_bwd_middle/ppermute | solution.py:37
  5.8 5.2 %collective-permute-start.8 = (bf16[1,128,4096]{2,1,0:T(8,128)(2,1)}, bf16[1,128,4096]{2,1,0:T(8,128)(2,1)S(1)}, u32[]{:S(2)}, u32[]{:S(2)}) collective-permute-start(bf16[1,128,4096]{2,1,0:T(8,128)(2,1)} %param.17), channel_id=1, source_target_pairs={{0,240},{16,0},{32,16},{48,32},{64,48},{80,64},{96,80},{112,96},{1... | collective-permute-start | bytes 3145736 | tf_op jit(solution)/shard_map/grad/ppermute | solution.py:37
  11.0 0.0 collective-permute-start
  11.0 0.7 %collective-permute-done.2.refs_1_.refs_5_ = bf16[1,128,1024]{2,1,0:T(8,128)(2,1)S(1)} collective-permute-done((bf16[1,128,1024]{2,1,0:T(8,128)(2,1)}, bf16[1,128,1024]{2,1,0:T(8,128)(2,1)S(1)}, u32[]{:S(2)}, u32[]{:S(2)}) %collective-permute-start.2) | collective-permute-done | bytes 262176 | tf_op jit(solution)/shard_map/kv_bwd_middle/ppermute | solution.py:37
  11.7 1.0 %broadcast_select_fusion.1 = bf16[1,128,1024]{2,1,0:T(8,128)(2,1)S(1)} fusion(bf16[1,128,1024]{2,1,0:T(8,128)(2,1)S(1)} %collective-permute-done.2.refs_1_.refs_5_, bf16[1,128,1024]{2,1,0:T(8,128)(2,1)} %get-tuple-element.21.refs_3_.refs_7_, pred[]{:T(512)S(6)} %eq.2), kind=kLoop, calls=%fused_computation.2 | loop fusion | flops 131072 | bytes 786433 | tf_op jit(solution)/shard_map/jit(_where)/select_n | solution.py:332
  12.7 0.1 collective-permute-start.4
  12.8 0.5 collective-permute-start.3
  13.3 9.5 %collective-permute-done.first_ref.refs_3_.refs_7_ = bf16[1,128,1152]{2,1,0:T(8,128)(2,1)S(1)} collective-permute-done((bf16[1,128,1152]{2,1,0:T(8,128)(2,1)}, bf16[1,128,1152]{2,1,0:T(8,128)(2,1)S(1)}, u32[]{:S(2)}, u32[]{:S(2)}) %collective-permute-start) | collective-permute-done | bytes 294944 | tf_op jit(solution)/shard_map/kv_moved/ppermute | solution.py:37
  22.7 0.0 collective-permute-start.1
  22.7 0.0 collective-permute-done.4.refs_2_.refs_6_
  22.7 0.0 collective-permute-done.3.refs_0_.refs_4_
  22.7 0.0 copy-start
  22.8 1.2 %copy-done = bf16[1,128,4096]{2,1,0:T(8,128)(2,1)S(1)} copy-done((bf16[1,128,4096]{2,1,0:T(8,128)(2,1)S(1)}, bf16[1,128,4096]{2,1,0:T(8,128)(2,1)}, u32[]{:S(2)}) %copy-start) | copy-done | bytes 1048600
  24.0 0.0 copy-start.2
  24.0 0.9 %copy-done.2 = bf16[1,128,1024]{2,1,0:T(8,128)(2,1)S(1)} copy-done((bf16[1,128,1024]{2,1,0:T(8,128)(2,1)S(1)}, bf16[1,128,1024]{2,1,0:T(8,128)(2,1)}, u32[]{:S(2)}) %copy-start.2) | copy-done | bytes 262168
  24.9 0.0 copy-start.3
  24.9 0.7 %copy-done.3 = s32[1,16]{1,0:T(1,128)S(1)} copy-done((s32[1,16]{1,0:T(1,128)S(1)}, s32[1,16]{1,0:T(1,128)}, u32[]{:S(2)}) %copy-start.3) | copy-done | bytes 88
  25.6 4.2 %shard_map.121.probs_ref = f32[4,1024,512]{2,1,0:T(8,128)S(1)} custom-call(s32[1,16]{1,0:T(1,128)S(1)} %copy-done.3, bf16[1,128,4096]{2,1,0:T(8,128)(2,1)S(1)} %copy-done, bf16[1,128,1024]{2,1,0:T(8,128)(2,1)S(1)} %collective-permute-done.3.refs_0_.refs_4_, bf16[1,128,1024]{2,1,0:T(8,128)(2,1)S(1)} %collective-permute-done.2.refs_1_.refs_5_, ...), custom_call_target="tpu_custom_call" | custom-call | flops 1 | bytes 1 | tf_op jit(solution)/shard_map/pallas_call | solution.py:251
  29.7 1.1 %collective-permute-start.5 = (bf16[1,128,1152]{2,1,0:T(8,128)(2,1)S(1)}, bf16[1,128,1152]{2,1,0:T(8,128)(2,1)S(1)}, u32[]{:S(2)}, u32[]{:S(2)}) collective-permute-start(bf16[1,128,1152]{2,1,0:T(8,128)(2,1)S(1)} %collective-permute-done.first_ref.refs_3_.refs_7_), channel_id=1, source_target_pairs={{0,2},{1,3},{2,4},{3,5},{4,6},{5,7},{6,8},{7,9},{8,10},{9,11},{10,... | collective-permute-start | bytes 884744 | tf_op jit(solution)/shard_map/kv_fwd_middle/ppermute | solution.py:37
  30.8 2.6 %collective-permute-done.8.grad_ref = bf16[1,128,4096]{2,1,0:T(8,128)(2,1)S(1)} collective-permute-done((bf16[1,128,4096]{2,1,0:T(8,128)(2,1)}, bf16[1,128,4096]{2,1,0:T(8,128)(2,1)S(1)}, u32[]{:S(2)}, u32[]{:S(2)}) %collective-permute-start.8) | collective-permute-done | bytes 1048608 | tf_op jit(solution)/shard_map/grad/ppermute | solution.py:37
  33.5 0.0 copy-done.1
  33.5 6.2 %shard_map.123 = (bf16[1,128,4096]{2,1,0:T(8,128)(2,1)}, bf16[1,128,1024]{2,1,0:T(8,128)(2,1)S(1)}, bf16[1,128,1024]{2,1,0:T(8,128)(2,1)S(1)}, bf16[1,128,1024]{...) custom-call(f32[4,1024,512]{2,1,0:T(8,128)S(1)} %shard_map.121.probs_ref, bf16[1,128,4096]{2,1,0:T(8,128)(2,1)S(1)} %copy-done.1, ...), custom_call_target="tpu_custom_call" | custom-call | flops 1 | bytes 1 | tf_op jit(solution)/shard_map/pallas_call | solution.py:273
  39.7 0.0 collective-permute-start.10
  39.7 0.5 collective-permute-start.9
  40.2 0.0 collective-permute-done.5.refs_1_.refs_5_
  40.3 0.1 collective-permute-start.7
  40.4 0.5 collective-permute-start.6
  40.9 2.7 %collective-permute-done.10 = bf16[1,128,1024]{2,1,0:T(8,128)(2,1)S(1)} collective-permute-done((bf16[1,128,1024]{2,1,0:T(8,128)(2,1)S(1)}, bf16[1,128,1024]{2,1,0:T(8,128)(2,1)S(1)}, u32[]{:S(2)}, u32[]{:S(2)}) %collective-permute-start.10) | collective-permute-done | bytes 262176 | tf_op jit(solution)/shard_map/part_far_0/ppermute | solution.py:37
  43.6 0.0 collective-permute-done.9.refs_1_
  43.6 0.1 add_convert_fusion
  43.7 5.9 %collective-permute-done.1.query_ref = bf16[1,128,4096]{2,1,0:T(8,128)(2,1)S(1)} collective-permute-done((bf16[1,128,4096]{2,1,0:T(8,128)(2,1)}, bf16[1,128,4096]{2,1,0:T(8,128)(2,1)S(1)}, u32[]{:S(2)}, u32[]{:S(2)}) %collective-permute-start.1) | collective-permute-done | bytes 1048608 | tf_op jit(solution)/shard_map/query_moved/ppermute | solution.py:37
  49.7 0.0 collective-permute-start.11
  49.7 0.0 collective-permute-done.7.refs_2_.refs_6_
  49.7 0.0 collective-permute-done.6.refs_0_.refs_4_
  49.7 5.2 %shard_map.122 = bf16[1,128,4096]{2,1,0:T(8,128)(2,1)} custom-call(bf16[1,128,1152]{2,1,0:T(8,128)(2,1)S(1)} %collective-permute-done.first_ref.refs_3_.refs_7_, bf16[1,128,4096]{2,1,0:T(8,128)(2,1)S(1)} %collective-permute-done.1.query_ref, bf16[1,128,1152]{2,1,0:T(8,128)(2,1)S(1)} %collective-permute-done.6.refs_0_.refs_4_, ...), custom_call_target="tpu_custom_call" | custom-call | flops 1 | bytes 1 | tf_op jit(solution)/shard_map/pallas_call | solution.py:232
  54.8 2.4 %collective-permute-done.11.refs_2_ = bf16[1,128,1024]{2,1,0:T(8,128)(2,1)S(1)} collective-permute-done((bf16[1,128,1024]{2,1,0:T(8,128)(2,1)S(1)}, bf16[1,128,1024]{2,1,0:T(8,128)(2,1)S(1)}, u32[]{:S(2)}, u32[]{:S(2)}) %collective-permute-start.11) | collective-permute-done | bytes 262176 | tf_op jit(solution)/shard_map/part_fold_0/ppermute | solution.py:37
  57.3 0.8 %shard_map.124 = (bf16[1,128,512]{2,1,0:T(8,128)(2,1)}, bf16[1,128,512]{2,1,0:T(8,128)(2,1)}) custom-call(bf16[1,128,1024]{2,1,0:T(8,128)(2,1)S(1)} %get-tuple-element.25.refs_0_, bf16[1,128,1024]{2,1,0:T(8,128)(2,1)S(1)} %collective-permute-done.9.refs_1_, bf16[1,128,1024]{2,1,0:T(8,128)(2,1)S(1)} %collective-permute-done.11.refs_2_), custom_call_target="tpu_custom_call" | custom-call | flops 1 | bytes 1 | tf_op jit(solution)/shard_map/pallas_call | solution.py:167
  (1 shorter events, 0.0 us)
Async XLA Ops:
  0.6 32.8 %copy-start.1 = (bf16[1,128,4096]{2,1,0:T(8,128)(2,1)S(1)}, bf16[1,128,4096]{2,1,0:T(8,128)(2,1)}, u32[]{:S(2)}) copy-start(bf16[1,128,4096]{2,1,0:T(8,128)(2,1)} %query_ref.3) | copy-start | bytes 3145732
  2.7 9.0 %collective-permute-start.2 = (bf16[1,128,1024]{2,1,0:T(8,128)(2,1)}, bf16[1,128,1024]{2,1,0:T(8,128)(2,1)S(1)}, u32[]{:S(2)}, u32[]{:S(2)}) collective-permute-start(bf16[1,128,1024]{2,1,0:T(8,128)(2,1)} %get-tuple-element.21.refs_3_.refs_7_), channel_id=1, source_target_pairs={{0,2},{1,3},{2,4},{3,5},{4,6},{5,7},{6,8},{7,9},{8,10},{9,11},{10,... | collective-permute-start | bytes 786440 | tf_op jit(solution)/shard_map/kv_bwd_middle/ppermute | solution.py:37
  5.8 27.7 %collective-permute-start.8 = (bf16[1,128,4096]{2,1,0:T(8,128)(2,1)}, bf16[1,128,4096]{2,1,0:T(8,128)(2,1)S(1)}, u32[]{:S(2)}, u32[]{:S(2)}) collective-permute-start(bf16[1,128,4096]{2,1,0:T(8,128)(2,1)} %param.17), channel_id=1, source_target_pairs={{0,240},{16,0},{32,16},{48,32},{64,48},{80,64},{96,80},{112,96},{1... | collective-permute-start | bytes 3145736 | tf_op jit(solution)/shard_map/grad/ppermute | solution.py:37
  11.0 11.7 %collective-permute-start = (bf16[1,128,1152]{2,1,0:T(8,128)(2,1)}, bf16[1,128,1152]{2,1,0:T(8,128)(2,1)S(1)}, u32[]{:S(2)}, u32[]{:S(2)}) collective-permute-start(bf16[1,128,1152]{2,1,0:T(8,128)(2,1)} %get-tuple-element.18), channel_id=1, source_target_pairs={{0,16},{16,32},{32,48},{48,64},{64,80},{80,96},{96,112},{112,128},... | collective-permute-start | bytes 884744 | tf_op jit(solution)/shard_map/kv_moved/ppermute | solution.py:37
  12.7 10.1 %collective-permute-start.4 = (bf16[1,128,1024]{2,1,0:T(8,128)(2,1)S(1)}, bf16[1,128,1024]{2,1,0:T(8,128)(2,1)S(1)}, u32[]{:S(2)}, u32[]{:S(2)}) collective-permute-start(bf16[1,128,1024]{2,1,0:T(8,128)(2,1)S(1)} %broadcast_select_fusion.1), channel_id=1, source_target_pairs={{0,1},{1,0},{2,3},{3,2},{4,5},{5,4},{6,7},{7,6},{8,9},{9,8},{10,11... | collective-permute-start | bytes 786440 | tf_op jit(solution)/shard_map/kv_bwd_near/ppermute | solution.py:43
  12.8 10.0 %collective-permute-start.3 = (bf16[1,128,1024]{2,1,0:T(8,128)(2,1)S(1)}, bf16[1,128,1024]{2,1,0:T(8,128)(2,1)S(1)}, u32[]{:S(2)}, u32[]{:S(2)}) collective-permute-start(bf16[1,128,1024]{2,1,0:T(8,128)(2,1)S(1)} %collective-permute-done.2.refs_1_.refs_5_), channel_id=1, source_target_pairs={{0,1},{1,2},{2,3},{3,4},{4,5},{5,6},{6,7},{7,8},{8,9},{9,10},{10,1... | collective-permute-start | bytes 786440 | tf_op jit(solution)/shard_map/kv_bwd_far/ppermute | solution.py:37
  22.7 26.9 %collective-permute-start.1 = (bf16[1,128,4096]{2,1,0:T(8,128)(2,1)}, bf16[1,128,4096]{2,1,0:T(8,128)(2,1)S(1)}, u32[]{:S(2)}, u32[]{:S(2)}) collective-permute-start(bf16[1,128,4096]{2,1,0:T(8,128)(2,1)} %param.9), channel_id=1, source_target_pairs={{0,16},{16,32},{32,48},{48,64},{64,80},{80,96},{96,112},{112,128},... | collective-permute-start | bytes 3145736 | tf_op jit(solution)/shard_map/query_moved/ppermute | solution.py:37
  22.7 1.2 %copy-start = (bf16[1,128,4096]{2,1,0:T(8,128)(2,1)S(1)}, bf16[1,128,4096]{2,1,0:T(8,128)(2,1)}, u32[]{:S(2)}) copy-start(bf16[1,128,4096]{2,1,0:T(8,128)(2,1)} %query_ref.3) | copy-start | bytes 3145732
  24.0 0.9 %copy-start.2 = (bf16[1,128,1024]{2,1,0:T(8,128)(2,1)S(1)}, bf16[1,128,1024]{2,1,0:T(8,128)(2,1)}, u32[]{:S(2)}) copy-start(bf16[1,128,1024]{2,1,0:T(8,128)(2,1)} %get-tuple-element.21.refs_3_.refs_7_) | copy-start | bytes 786436
  24.9 0.7 %copy-start.3 = (s32[1,16]{1,0:T(1,128)S(1)}, s32[1,16]{1,0:T(1,128)}, u32[]{:S(2)}) copy-start(s32[1,16]{1,0:T(1,128)} %len_ref.3) | copy-start | bytes 196
  29.7 10.5 %collective-permute-start.5 = (bf16[1,128,1152]{2,1,0:T(8,128)(2,1)S(1)}, bf16[1,128,1152]{2,1,0:T(8,128)(2,1)S(1)}, u32[]{:S(2)}, u32[]{:S(2)}) collective-permute-start(bf16[1,128,1152]{2,1,0:T(8,128)(2,1)S(1)} %collective-permute-done.first_ref.refs_3_.refs_7_), channel_id=1, source_target_pairs={{0,2},{1,3},{2,4},{3,5},{4,6},{5,7},{6,8},{7,9},{8,10},{9,11},{10,... | collective-permute-start | bytes 884744 | tf_op jit(solution)/shard_map/kv_fwd_middle/ppermute | solution.py:37
  39.7 3.9 %collective-permute-start.10 = (bf16[1,128,1024]{2,1,0:T(8,128)(2,1)S(1)}, bf16[1,128,1024]{2,1,0:T(8,128)(2,1)S(1)}, u32[]{:S(2)}, u32[]{:S(2)}) collective-permute-start(bf16[1,128,1024]{2,1,0:T(8,128)(2,1)S(1)} %get-tuple-element.28), channel_id=1, source_target_pairs={{0,15},{1,0},{2,1},{3,2},{4,3},{5,4},{6,5},{7,6},{8,7},{9,8},{10,9... | collective-permute-start | bytes 786440 | tf_op jit(solution)/shard_map/part_far_0/ppermute | solution.py:37
  39.7 3.9 %collective-permute-start.9 = (bf16[1,128,1024]{2,1,0:T(8,128)(2,1)S(1)}, bf16[1,128,1024]{2,1,0:T(8,128)(2,1)S(1)}, u32[]{:S(2)}, u32[]{:S(2)}) collective-permute-start(bf16[1,128,1024]{2,1,0:T(8,128)(2,1)S(1)} %get-tuple-element.26), channel_id=1, source_target_pairs={{0,1},{1,0},{2,3},{3,2},{4,5},{5,4},{6,7},{7,6},{8,9},{9,8},{10,11... | collective-permute-start | bytes 786440 | tf_op jit(solution)/shard_map/part_near_0/ppermute | solution.py:43
  40.3 9.4 %collective-permute-start.7 = (bf16[1,128,1152]{2,1,0:T(8,128)(2,1)S(1)}, bf16[1,128,1152]{2,1,0:T(8,128)(2,1)S(1)}, u32[]{:S(2)}, u32[]{:S(2)}) collective-permute-start(bf16[1,128,1152]{2,1,0:T(8,128)(2,1)S(1)} %broadcast_select_fusion), channel_id=1, source_target_pairs={{0,1},{1,0},{2,3},{3,2},{4,5},{5,4},{6,7},{7,6},{8,9},{9,8},{10,11... | collective-permute-start | bytes 884744 | tf_op jit(solution)/shard_map/kv_fwd_near/ppermute | solution.py:43
  40.4 9.3 %collective-permute-start.6 = (bf16[1,128,1152]{2,1,0:T(8,128)(2,1)S(1)}, bf16[1,128,1152]{2,1,0:T(8,128)(2,1)S(1)}, u32[]{:S(2)}, u32[]{:S(2)}) collective-permute-start(bf16[1,128,1152]{2,1,0:T(8,128)(2,1)S(1)} %collective-permute-done.5.refs_1_.refs_5_), channel_id=1, source_target_pairs={{0,1},{1,2},{2,3},{3,4},{4,5},{5,6},{6,7},{7,8},{8,9},{9,10},{10,1... | collective-permute-start | bytes 884744 | tf_op jit(solution)/shard_map/kv_fwd_far/ppermute | solution.py:37
  49.7 7.6 %collective-permute-start.11 = (bf16[1,128,1024]{2,1,0:T(8,128)(2,1)S(1)}, bf16[1,128,1024]{2,1,0:T(8,128)(2,1)S(1)}, u32[]{:S(2)}, u32[]{:S(2)}) collective-permute-start(bf16[1,128,1024]{2,1,0:T(8,128)(2,1)S(1)} %add_convert_fusion), channel_id=1, source_target_pairs={{0,14},{1,15},{2,0},{3,1},{4,2},{5,3},{6,4},{7,5},{8,6},{9,7},{10,... | collective-permute-start | bytes 786440 | tf_op jit(solution)/shard_map/part_fold_0/ppermute | solution.py:37

commit v3 on v2

--- a/solution.py
+++ b/solution.py
@@ -20,8 +20,6 @@
 MASKED = -1e30
 KV_WIDTH = KV_HEADS * HEAD_DIM
 GROUP_WIDTH = GROUP * HEAD_DIM
-CHUNKS = (4,)
-FOLDS = ((0,),)
 HEADS_AT_ONCE = 4
 VMEM = 24 * 1024 * 1024
 COST = 1
@@ -134,8 +132,8 @@
 def backward_kernel(probs_ref, query_ref, grad_ref, *refs):
     key_refs, value_refs = refs[:4], refs[4:8]
     (
-        out_ref, own_ref, middle_ref, near_ref, far_ref, queries_ref, grads_ref, scores_ref, low_ref
-    ) = refs[-9:]
+        scores_ref, own_ref, middle_ref, near_ref, far_ref, queries_ref, grads_ref, low_ref
+    ) = refs[-8:]
     last = lax.axis_size("section") - 1
     keep = (lax.axis_index("section") < last).astype(jnp.float32).astype(jnp.bfloat16)
     keys, values = stacked(key_refs), stacked(value_refs)
@@ -146,19 +144,24 @@
         probs = probs_ref[0, at, :]
         d_prob = lax.dot_general(grads_ref[at, :], values, NT, preferred_element_type=jnp.float32)
         delta = jnp.sum(probs * d_prob, axis=1, keepdims=True)
-        scores_ref[at, :] = (probs * (d_prob - delta)).astype(jnp.bfloat16)
+        scores_ref[0, at, :] = (probs * (d_prob - delta)).astype(jnp.bfloat16)
         low_ref[at, :] = probs.astype(jnp.bfloat16)
-    d_query = jnp.dot(scores_ref[...], keys, preferred_element_type=jnp.float32) * SCALE
-    for index in range(GROUP):
-        out_ref[0, :, head(index)] = d_query[index * ROWS : (index + 1) * ROWS].astype(
-            jnp.bfloat16
-        )
-    d_key = jnp.dot(queries_ref[...].T, scores_ref[...], preferred_element_type=jnp.float32).T
+    d_key = jnp.dot(queries_ref[...].T, scores_ref[0], preferred_element_type=jnp.float32).T
     d_value = jnp.dot(grads_ref[...].T, low_ref[...], preferred_element_type=jnp.float32).T
     for piece, part_ref in enumerate((far_ref, middle_ref, near_ref, own_ref)):
         at = slice(piece * ROWS, (piece + 1) * ROWS)
         part_ref[0, :, :HEAD_DIM] = (d_key[at] * SCALE).astype(jnp.bfloat16)
         part_ref[0, :, HEAD_DIM:] = d_value[at].astype(jnp.bfloat16)
+
+
+def query_kernel(scores_ref, *refs):
+    key_refs, out_ref = refs[:4], refs[4]
+    keys = stacked(key_refs)
+    d_query = jnp.dot(scores_ref[0], keys, preferred_element_type=jnp.float32) * SCALE
+    for index in range(GROUP):
+        out_ref[0, :, head(index)] = d_query[index * ROWS : (index + 1) * ROWS].astype(
+            jnp.bfloat16
+        )
 
 
 def small_call(
@@ -207,13 +210,10 @@
     )
 
 
-def folded(middles, fars, nears):
-    sums = []
-    for middle, far, near in zip(middles, fars, nears):
-        total = middle.astype(jnp.float32) + far.astype(jnp.float32)
-        total = total + jnp.where(second_core(), near.astype(jnp.float32), 0.0)
-        sums.append(total.astype(jnp.bfloat16))
-    return sums[0] if len(sums) == 1 else jnp.concatenate(sums, axis=2)
+def folded(middle, far, near):
+    total = middle.astype(jnp.float32) + far.astype(jnp.float32)
+    total = total + jnp.where(second_core(), near.astype(jnp.float32), 0.0)
+    return total.astype(jnp.bfloat16)
 
 
 def group_spec(first):
@@ -260,59 +260,49 @@
     )(lengths, query, *pieces)
 
 
-def backward(probs, query, out_grad, pieces, first, groups, so_far):
-    width = groups * 2 * HEAD_DIM
-    in_specs = [pl.BlockSpec((1, GROUP * ROWS, KEYS), lambda i: (first + i, 0, 0))]
-    in_specs += [group_spec(first)] * 2 + key_specs(first) + value_specs(first)
-    operands = [probs, query, out_grad, *pieces, *pieces]
-    aliases = {}
-    if so_far is not None:
-        in_specs.append(pl.BlockSpec(memory_space=pl.ANY))
-        aliases = {len(operands): 0}
-        operands.append(so_far)
-    result = pl.pallas_call(
+def backward(probs, query, out_grad, pieces):
+    block = (1, GROUP * ROWS, KEYS)
+    return pl.pallas_call(
         backward_kernel,
-        grid=(groups,),
-        out_shape=[jax.ShapeDtypeStruct(query.shape, jnp.bfloat16)]
-        + [jax.ShapeDtypeStruct((1, ROWS, width), jnp.bfloat16)] * 4,
-        in_specs=in_specs,
-        out_specs=[group_spec(first)]
+        grid=(KV_HEADS,),
+        out_shape=[jax.ShapeDtypeStruct(probs.shape, jnp.bfloat16)]
+        + [jax.ShapeDtypeStruct((1, ROWS, 2 * KV_WIDTH), jnp.bfloat16)] * 4,
+        in_specs=[pl.BlockSpec(block, lambda i: (i, 0, 0))]
+        + [group_spec(0)] * 2
+        + key_specs(0)
+        + value_specs(0),
+        out_specs=[pl.BlockSpec(block, lambda i: (i, 0, 0))]
         + [pl.BlockSpec((1, ROWS, 2 * HEAD_DIM), lambda i: (0, 0, i))] * 4,
         scratch_shapes=[
             pltpu.VMEM((GROUP * ROWS, HEAD_DIM), jnp.bfloat16),
             pltpu.VMEM((GROUP * ROWS, HEAD_DIM), jnp.bfloat16),
             pltpu.VMEM((GROUP * ROWS, KEYS), jnp.bfloat16),
-            pltpu.VMEM((GROUP * ROWS, KEYS), jnp.bfloat16),
         ],
-        input_output_aliases=aliases,
         cost_estimate=cost(COST, COST),
         compiler_params=params(VMEM),
-    )(*operands)
-    return result[0], result[1:]
-
-
-def add_kernel(*refs):
-    chunks = len(CHUNKS)
-    own_refs, near_refs, fold_refs = refs[:chunks], refs[chunks : 2 * chunks], refs[2 * chunks : -2]
-    key_ref, value_ref = refs[-2:]
-    folds = [
-        (ref, at)
-        for ref, members in zip(fold_refs, FOLDS)
-        for at in [sum(CHUNKS[chunk] for chunk in members[:spot]) for spot in range(len(members))]
-    ]
-    first = 0
+    )(probs, query, out_grad, *pieces, *pieces)
+
+
+def query_gradient(scores, pieces):
+    return pl.pallas_call(
+        query_kernel,
+        grid=(KV_HEADS,),
+        out_shape=jax.ShapeDtypeStruct((1, ROWS, HEADS * HEAD_DIM), jnp.bfloat16),
+        in_specs=[pl.BlockSpec((1, GROUP * ROWS, KEYS), lambda i: (i, 0, 0))] + key_specs(0),
+        out_specs=group_spec(0),
+        cost_estimate=cost(COST, COST),
+        compiler_params=params(VMEM),
+    )(scores, *pieces)
+
+
+def add_kernel(own_ref, near_ref, fold_ref, key_ref, value_ref):
     first_core = lax.rem(lax.axis_index("ctx"), 2) == 0
-    for groups, own_ref, near_ref, (fold_ref, at) in zip(CHUNKS, own_refs, near_refs, folds):
-        for group in range(groups):
-            here = slice(2 * group * HEAD_DIM, 2 * (group + 1) * HEAD_DIM)
-            there = slice(2 * (at + group) * HEAD_DIM, 2 * (at + group + 1) * HEAD_DIM)
-            total = own_ref[0, :, here].astype(jnp.float32)
-            near = near_ref[0, :, here].astype(jnp.float32)
-            total = total + jnp.where(first_core, near, 0.0)
-            total = (total + fold_ref[0, :, there].astype(jnp.float32)).astype(jnp.bfloat16)
-            key_ref[0, :, head(first + group)] = total[:, :HEAD_DIM]
-            value_ref[0, :, head(first + group)] = total[:, HEAD_DIM:]
-        first += groups
+    total = own_ref[0].astype(jnp.float32) + fold_ref[0].astype(jnp.float32)
+    total = total + jnp.where(first_core, near_ref[0].astype(jnp.float32), 0.0)
+    total = total.astype(jnp.bfloat16)
+    for group in range(KV_HEADS):
+        key_ref[0, :, head(group)] = total[:, head(2 * group)]
+        value_ref[0, :, head(group)] = total[:, head(2 * group + 1)]
 
 
 def add_parts(*parts):
@@ -328,9 +318,12 @@
 
 def gather_behind(own, what, *earlier):
     middle = from_behind(after(own, *earlier), "ctx", 2, what + "_middle")
-    far = from_behind(middle, "ctx", 1, what + "_far")
-    near = swapped(jnp.where(second_core(), middle, own), what + "_near")
-    return far, middle, near, own
+    return from_behind(middle, "ctx", 1, what + "_far"), middle
+
+
+def shared_behind(own, middle, what, *earlier):
+    shared = jnp.where(second_core(), middle, own)
+    return swapped(after(shared, *earlier), what + "_near")
 
 
 def on_device(
@@ -347,31 +340,21 @@
     out_grad = from_behind(grad_held, "section", -1, "grad")
     kv_fwd, own_bwd = pack(doc_len_fwd, key_fwd, value_fwd, key_bwd, value_bwd)
     own_fwd = from_behind(kv_fwd, "section", 1, "kv_moved")
-    pieces_bwd = gather_behind(own_bwd, "kv_bwd", kv_fwd)
+    far_bwd, middle_bwd = gather_behind(own_bwd, "kv_bwd", kv_fwd)
+    near_bwd = shared_behind(own_bwd, middle_bwd, "kv_bwd")
+    pieces_bwd = (far_bwd, middle_bwd, near_bwd, own_bwd)
     query_moved = from_behind(after(query_fwd, own_fwd), "section", 1, "query_moved")
     probs = probabilities(doc_len_bwd, query_bwd, pieces_bwd)
-    pieces_fwd = gather_behind(own_fwd, "kv_fwd", probs)
-    grad_query = None
-    first = 0
-    owns, middles, nears, fars, folds = [], [], [], [], []
-    for chunk, groups in enumerate(CHUNKS):
-        grad_query, (own, middle, near, far) = backward(
-            probs, query_bwd, out_grad, pieces_bwd, first, groups, grad_query
-        )
-        first += groups
-        if chunk > 0:
-            far = after(far, fars[0])
-        owns.append(own)
-        middles.append(middle)
-        fars.append(from_behind(far, "ctx", -1, f"part_far_{chunk}"))
-        nears.append(swapped(near, f"part_near_{chunk}"))
-    for members in FOLDS:
-        fold = folded(*([values[chunk] for chunk in members] for values in (middles, fars, nears)))
-        if members == FOLDS[-1]:
-            fold = after(fold, query_moved)
-        folds.append(from_behind(fold, "ctx", -2, f"part_fold_{members[0]}"))
-    next_stream = forward(query_moved, pieces_fwd)
-    grad_key, grad_value = add_parts(after(owns[0], next_stream), *owns[1:], *nears, *folds)
+    far_fwd, middle_fwd = gather_behind(own_fwd, "kv_fwd", probs, out_grad, own_fwd)
+    scores, own, middle, near, far = backward(probs, query_bwd, out_grad, pieces_bwd)
+    far = from_behind(far, "ctx", -1, "part_far")
+    near = swapped(near, "part_near")
+    grad_query = query_gradient(scores, pieces_bwd)
+    fold = after(folded(middle, far, near), grad_query, query_moved)
+    near_fwd = shared_behind(own_fwd, middle_fwd, "kv_fwd")
+    fold = from_behind(fold, "ctx", -2, "part_fold")
+    next_stream = forward(query_moved, (far_fwd, middle_fwd, near_fwd, own_fwd))
+    grad_key, grad_value = add_parts(after(own, next_stream), near, fold)
     return (next_stream, grad_query, grad_key, grad_value)
 
 

time: 58.3 us -> 58.6 us (level)
  waiting for transfers between devices: 23.9 us -> 19 us
  starting transfers between devices: 11.1 us -> 15 us
  Pallas kernels: 18.4 us -> 19.8 us
    ppermute x9, waiting for transfers between devices: 23.9 us -> 19 us  [from_behind(): lax.ppermute(value, axis, [(at, (at + steps) % count) for at in range(cou...]
    ppermute x9, starting transfers between devices: 10.4 us -> 14.2 us  [from_behind(): lax.ppermute(value, axis, [(at, (at + steps) % count) for at in range(cou...]
    pallas_call x1 -> x2, Pallas kernels: 6.25 us -> 7.69 us  [the longest x1 4.83 us: backward(): pl.pallas_call(backward_kernel, grid=(KV_HEADS,), out_shape=[jax.ShapeDty...]
  transfers between devices with their start and end apart: 12 -> 12, of which waited for: 6 -> 5; matrix products, arithmetic and copies ran while one was open for 2% -> 2% of each run, Pallas kernels for 27% -> 32%
where the time goes in v3:
time: 58.6 us; the launch traced here: 58.4 us
  Pallas kernels  19.8 us (34%)
  waiting for transfers between devices  19 us (32%)
  starting transfers between devices  15 us (26%)
  local copies, waits for them, and re-layouts  2.84 us (5%)
  other arithmetic  1.14 us (2%)
  between operations  0.71 us (1%)
    ppermute x9, waiting for transfers between devices, from_behind(): lax.ppermute(value, axis, [(at, (at + steps) % count) for at in range(cou...  19 us
    ppermute x9, starting transfers between devices, from_behind(): lax.ppermute(value, axis, [(at, (at + steps) % count) for at in range(cou...  14.2 us
    pallas_call x1, Pallas kernels, forward(): pl.pallas_call(forward_kernel, grid=(KV_HEADS,), out_shape=jax.ShapeDtype...  5.16 us
    pallas_call x1, Pallas kernels, backward(): pl.pallas_call(backward_kernel, grid=(KV_HEADS,), out_shape=[jax.ShapeDty...  4.83 us
    pallas_call x1, Pallas kernels, probabilities(): pl.pallas_call(probs_kernel, grid=(KV_HEADS,), out_shape=jax.ShapeDtypeSt...  4.15 us
    pallas_call x1, Pallas kernels, query_gradient(): pl.pallas_call(query_kernel, grid=(KV_HEADS,), out_shape=jax.ShapeDtypeSt...  2.85 us
    unnamed x8, local copies, waits for them, and re-layouts  2.84 us
    pallas_call x2, Pallas kernels, small_call(): pl.pallas_call(kernel, grid=(steps,), out_shape=[jax.ShapeDtypeStruct(sha...  2.77 us
  transfers between devices with their start and end apart: 12, of which 5 were waited for; matrix products, arithmetic and copies ran while one was open for 2% of the time, Pallas kernels for 32%

profile of v3, /device:TPU:96, one launch (start us, length us, event | category | flops | bytes accessed | tf_op | source)
XLA Modules:
  0.0 58.4 jit_solution(3730475086111779725)
XLA Ops:
  0.6 0.0 copy-start.2
  0.6 5.3 %collective-permute-start.5 = (bf16[1,128,4096]{2,1,0:T(8,128)(2,1)}, bf16[1,128,4096]{2,1,0:T(8,128)(2,1)S(1)}, u32[]{:S(2)}, u32[]{:S(2)}) collective-permute-start(bf16[1,128,4096]{2,1,0:T(8,128)(2,1)} %param.17), channel_id=1, source_target_pairs={{0,240},{16,0},{32,16},{48,32},{64,48},{80,64},{96,80},{112,96},{1... | collective-permute-start | bytes 3145736 | tf_op jit(solution)/shard_map/grad/ppermute | solution.py:35
  5.9 1.9 %shard_map.120 = (bf16[1,128,1152]{2,1,0:T(8,128)(2,1)}, bf16[1,128,1024]{2,1,0:T(8,128)(2,1)}) custom-call(s32[1,16]{1,0:T(1,128)} %len_ref.2, bf16[1,128,512]{2,1,0:T(8,128)(2,1)} %key_fwd.1, bf16[1,128,512]{2,1,0:T(8,128)(2,1)} %value_fwd.1, bf16[1,128,512]{2,1,0:T(8,128)(2,1)} %key_bwd.1, bf16[1,128,512]{2,1,0:T(8,128)(2,1)} %value_bwd.1), custom_call_target="tpu_custom_call" | custom-call | flops 1 | bytes 1 | tf_op jit(solution)/shard_map/pallas_call | solution.py:170
  7.9 3.1 %collective-permute-start.2 = (bf16[1,128,1024]{2,1,0:T(8,128)(2,1)}, bf16[1,128,1024]{2,1,0:T(8,128)(2,1)S(1)}, u32[]{:S(2)}, u32[]{:S(2)}) collective-permute-start(bf16[1,128,1024]{2,1,0:T(8,128)(2,1)} %get-tuple-element.21.refs_3_.refs_7_), channel_id=1, source_target_pairs={{0,2},{1,3},{2,4},{3,5},{4,6},{5,7},{6,8},{7,9},{8,10},{9,11},{10,... | collective-permute-start | bytes 786440 | tf_op jit(solution)/shard_map/kv_bwd_middle/ppermute | solution.py:35
  11.0 0.0 collective-permute-start
  11.0 5.6 %collective-permute-done.2.refs_1_.refs_5_ = bf16[1,128,1024]{2,1,0:T(8,128)(2,1)S(1)} collective-permute-done((bf16[1,128,1024]{2,1,0:T(8,128)(2,1)}, bf16[1,128,1024]{2,1,0:T(8,128)(2,1)S(1)}, u32[]{:S(2)}, u32[]{:S(2)}) %collective-permute-start.2) | collective-permute-done | bytes 262176 | tf_op jit(solution)/shard_map/kv_bwd_middle/ppermute | solution.py:35
  16.6 1.0 %broadcast_select_fusion.1 = bf16[1,128,1024]{2,1,0:T(8,128)(2,1)S(1)} fusion(bf16[1,128,1024]{2,1,0:T(8,128)(2,1)S(1)} %collective-permute-done.2.refs_1_.refs_5_, bf16[1,128,1024]{2,1,0:T(8,128)(2,1)} %get-tuple-element.21.refs_3_.refs_7_, pred[]{:T(512)S(6)} %eq.2), kind=kLoop, calls=%fused_computation.2 | loop fusion | flops 131072 | bytes 786433 | tf_op jit(solution)/shard_map/jit(_where)/select_n | solution.py:325
  17.6 0.1 collective-permute-start.4
  17.7 0.5 collective-permute-start.3
  18.2 4.5 %collective-permute-done.first_ref.refs_3_.refs_7_ = bf16[1,128,1152]{2,1,0:T(8,128)(2,1)S(1)} collective-permute-done((bf16[1,128,1152]{2,1,0:T(8,128)(2,1)}, bf16[1,128,1152]{2,1,0:T(8,128)(2,1)S(1)}, u32[]{:S(2)}, u32[]{:S(2)}) %collective-permute-start) | collective-permute-done | bytes 294944 | tf_op jit(solution)/shard_map/kv_moved/ppermute | solution.py:35
  22.7 0.0 collective-permute-start.1
  22.7 0.0 collective-permute-done.4.refs_2_.refs_6_
  22.7 0.8 %collective-permute-done.3.refs_0_.refs_4_ = bf16[1,128,1024]{2,1,0:T(8,128)(2,1)S(1)} collective-permute-done((bf16[1,128,1024]{2,1,0:T(8,128)(2,1)S(1)}, bf16[1,128,1024]{2,1,0:T(8,128)(2,1)S(1)}, u32[]{:S(2)}, u32[]{:S(2)}) %collective-permute-start.3) | collective-permute-done | bytes 262176 | tf_op jit(solution)/shard_map/kv_bwd_far/ppermute | solution.py:35
  23.5 0.0 copy-start
  23.5 0.9 %copy-done = bf16[1,128,1024]{2,1,0:T(8,128)(2,1)S(1)} copy-done((bf16[1,128,1024]{2,1,0:T(8,128)(2,1)S(1)}, bf16[1,128,1024]{2,1,0:T(8,128)(2,1)}, u32[]{:S(2)}) %copy-start) | copy-done | bytes 262168
  24.4 0.0 copy-start.1
  24.4 1.2 %copy-done.1 = bf16[1,128,4096]{2,1,0:T(8,128)(2,1)S(1)} copy-done((bf16[1,128,4096]{2,1,0:T(8,128)(2,1)S(1)}, bf16[1,128,4096]{2,1,0:T(8,128)(2,1)}, u32[]{:S(2)}) %copy-start.1) | copy-done | bytes 1048600
  25.7 0.0 copy-start.3
  25.7 0.7 %copy-done.3 = s32[1,16]{1,0:T(1,128)S(1)} copy-done((s32[1,16]{1,0:T(1,128)S(1)}, s32[1,16]{1,0:T(1,128)}, u32[]{:S(2)}) %copy-start.3) | copy-done | bytes 88
  26.3 4.2 %shard_map.121.probs_ref = f32[4,1024,512]{2,1,0:T(8,128)S(1)} custom-call(s32[1,16]{1,0:T(1,128)S(1)} %copy-done.3, bf16[1,128,4096]{2,1,0:T(8,128)(2,1)S(1)} %copy-done.1, bf16[1,128,1024]{2,1,0:T(8,128)(2,1)S(1)} %collective-permute-done.3.refs_0_.refs_4_, bf16[1,128,1024]{2,1,0:T(8,128)(2,1)S(1)} %collective-permute-done.2.refs_1_.refs_5_, ...), custom_call_target="tpu_custom_call" | custom-call | flops 1 | bytes 1 | tf_op jit(solution)/shard_map/pallas_call | solution.py:251
  30.5 0.0 collective-permute-done.5.grad_ref
  30.5 4.9 %collective-permute-start.6 = (bf16[1,128,1152]{2,1,0:T(8,128)(2,1)S(1)}, bf16[1,128,1152]{2,1,0:T(8,128)(2,1)S(1)}, u32[]{:S(2)}, u32[]{:S(2)}) collective-permute-start(bf16[1,128,1152]{2,1,0:T(8,128)(2,1)S(1)} %collective-permute-done.first_ref.refs_3_.refs_7_), channel_id=1, source_target_pairs={{0,2},{1,3},{2,4},{3,5},{4,6},{5,7},{6,8},{7,9},{8,10},{9,11},{10,... | collective-permute-start | bytes 884744 | tf_op jit(solution)/shard_map/kv_fwd_middle/ppermute | solution.py:35
  35.4 0.0 copy-done.2
  35.4 4.8 %shard_map.123 = (bf16[4,1024,512]{2,1,0:T(8,128)(2,1)S(1)}, bf16[1,128,1024]{2,1,0:T(8,128)(2,1)S(1)}, bf16[1,128,1024]{2,1,0:T(8,128)(2,1)S(1)}, bf16[1,128,10...) custom-call(f32[4,1024,512]{2,1,0:T(8,128)S(1)} %shard_map.121.probs_ref, bf16[1,128,4096]{2,1,0:T(8,128)(2,1)S(1)} %copy-done.2, ...), custom_call_target="tpu_custom_call" | custom-call | flops 1 | bytes 1 | tf_op jit(solution)/shard_map/pallas_call | solution.py:265
  40.2 0.0 collective-permute-start.10
  40.2 0.5 collective-permute-start.9
  40.7 2.9 %shard_map.124 = bf16[1,128,4096]{2,1,0:T(8,128)(2,1)} custom-call(bf16[4,1024,512]{2,1,0:T(8,128)(2,1)S(1)} %get-tuple-element.23.scores_ref, bf16[1,128,1024]{2,1,0:T(8,128)(2,1)S(1)} %collective-permute-done.3.refs_0_.refs_4_, bf16[1,128,1024]{2,1,0:T(8,128)(2,1)S(1)} %collective-permute-done.2.refs_1_.refs_5_, ...), custom_call_target="tpu_custom_call" | custom-call | flops 1 | bytes 1 | tf_op jit(solution)/shard_map/pallas_call | solution.py:287
  43.6 0.0 collective-permute-done.6.refs_1_.refs_5_
  43.6 0.2 collective-permute-start.8
  43.8 0.4 collective-permute-start.7
  44.2 0.0 collective-permute-done.10
  44.2 0.0 collective-permute-done.9.near_ref
  44.2 0.1 add_convert_fusion
  44.4 5.6 %collective-permute-done.1.query_ref = bf16[1,128,4096]{2,1,0:T(8,128)(2,1)S(1)} collective-permute-done((bf16[1,128,4096]{2,1,0:T(8,128)(2,1)}, bf16[1,128,4096]{2,1,0:T(8,128)(2,1)S(1)}, u32[]{:S(2)}, u32[]{:S(2)}) %collective-permute-start.1) | collective-permute-done | bytes 1048608 | tf_op jit(solution)/shard_map/query_moved/ppermute | solution.py:35
  50.0 0.0 collective-permute-start.11
  50.0 0.0 collective-permute-done.8.refs_2_.refs_6_
  50.0 0.0 collective-permute-done.7.refs_0_.refs_4_
  50.0 5.2 %shard_map.122 = bf16[1,128,4096]{2,1,0:T(8,128)(2,1)} custom-call(bf16[1,128,1152]{2,1,0:T(8,128)(2,1)S(1)} %collective-permute-done.first_ref.refs_3_.refs_7_, bf16[1,128,4096]{2,1,0:T(8,128)(2,1)S(1)} %collective-permute-done.1.query_ref, bf16[1,128,1152]{2,1,0:T(8,128)(2,1)S(1)} %collective-permute-done.7.refs_0_.refs_4_, ...), custom_call_target="tpu_custom_call" | custom-call | flops 1 | bytes 1 | tf_op jit(solution)/shard_map/pallas_call | solution.py:232
  55.2 2.4 %collective-permute-done.11.fold_ref = bf16[1,128,1024]{2,1,0:T(8,128)(2,1)S(1)} collective-permute-done((bf16[1,128,1024]{2,1,0:T(8,128)(2,1)S(1)}, bf16[1,128,1024]{2,1,0:T(8,128)(2,1)S(1)}, u32[]{:S(2)}, u32[]{:S(2)}) %collective-permute-start.11) | collective-permute-done | bytes 262176 | tf_op jit(solution)/shard_map/part_fold/ppermute | solution.py:35
  57.6 0.8 %shard_map.125 = (bf16[1,128,512]{2,1,0:T(8,128)(2,1)}, bf16[1,128,512]{2,1,0:T(8,128)(2,1)}) custom-call(bf16[1,128,1024]{2,1,0:T(8,128)(2,1)S(1)} %get-tuple-element.25.own_ref, bf16[1,128,1024]{2,1,0:T(8,128)(2,1)S(1)} %collective-permute-done.9.near_ref, bf16[1,128,1024]{2,1,0:T(8,128)(2,1)S(1)} %collective-permute-done.11.fold_ref), custom_call_target="tpu_custom_call" | custom-call | flops 1 | bytes 1 | tf_op jit(solution)/shard_map/pallas_call | solution.py:170
  (1 shorter events, 0.0 us)
Async XLA Ops:
  0.6 34.7 %copy-start.2 = (bf16[1,128,4096]{2,1,0:T(8,128)(2,1)S(1)}, bf16[1,128,4096]{2,1,0:T(8,128)(2,1)}, u32[]{:S(2)}) copy-start(bf16[1,128,4096]{2,1,0:T(8,128)(2,1)} %query_ref.3) | copy-start | bytes 3145732
  0.6 29.8 %collective-permute-start.5 = (bf16[1,128,4096]{2,1,0:T(8,128)(2,1)}, bf16[1,128,4096]{2,1,0:T(8,128)(2,1)S(1)}, u32[]{:S(2)}, u32[]{:S(2)}) collective-permute-start(bf16[1,128,4096]{2,1,0:T(8,128)(2,1)} %param.17), channel_id=1, source_target_pairs={{0,240},{16,0},{32,16},{48,32},{64,48},{80,64},{96,80},{112,96},{1... | collective-permute-start | bytes 3145736 | tf_op jit(solution)/shard_map/grad/ppermute | solution.py:35
  7.9 8.7 %collective-permute-start.2 = (bf16[1,128,1024]{2,1,0:T(8,128)(2,1)}, bf16[1,128,1024]{2,1,0:T(8,128)(2,1)S(1)}, u32[]{:S(2)}, u32[]{:S(2)}) collective-permute-start(bf16[1,128,1024]{2,1,0:T(8,128)(2,1)} %get-tuple-element.21.refs_3_.refs_7_), channel_id=1, source_target_pairs={{0,2},{1,3},{2,4},{3,5},{4,6},{5,7},{6,8},{7,9},{8,10},{9,11},{10,... | collective-permute-start | bytes 786440 | tf_op jit(solution)/shard_map/kv_bwd_middle/ppermute | solution.py:35
  11.0 11.7 %collective-permute-start = (bf16[1,128,1152]{2,1,0:T(8,128)(2,1)}, bf16[1,128,1152]{2,1,0:T(8,128)(2,1)S(1)}, u32[]{:S(2)}, u32[]{:S(2)}) collective-permute-start(bf16[1,128,1152]{2,1,0:T(8,128)(2,1)} %get-tuple-element.18), channel_id=1, source_target_pairs={{0,16},{16,32},{32,48},{48,64},{64,80},{80,96},{96,112},{112,128},... | collective-permute-start | bytes 884744 | tf_op jit(solution)/shard_map/kv_moved/ppermute | solution.py:35
  17.6 5.1 %collective-permute-start.4 = (bf16[1,128,1024]{2,1,0:T(8,128)(2,1)S(1)}, bf16[1,128,1024]{2,1,0:T(8,128)(2,1)S(1)}, u32[]{:S(2)}, u32[]{:S(2)}) collective-permute-start(bf16[1,128,1024]{2,1,0:T(8,128)(2,1)S(1)} %broadcast_select_fusion.1), channel_id=1, source_target_pairs={{0,1},{1,0},{2,3},{3,2},{4,5},{5,4},{6,7},{7,6},{8,9},{9,8},{10,11... | collective-permute-start | bytes 786440 | tf_op jit(solution)/shard_map/kv_bwd_near/ppermute | solution.py:41
  17.7 5.8 %collective-permute-start.3 = (bf16[1,128,1024]{2,1,0:T(8,128)(2,1)S(1)}, bf16[1,128,1024]{2,1,0:T(8,128)(2,1)S(1)}, u32[]{:S(2)}, u32[]{:S(2)}) collective-permute-start(bf16[1,128,1024]{2,1,0:T(8,128)(2,1)S(1)} %collective-permute-done.2.refs_1_.refs_5_), channel_id=1, source_target_pairs={{0,1},{1,2},{2,3},{3,4},{4,5},{5,6},{6,7},{7,8},{8,9},{9,10},{10,1... | collective-permute-start | bytes 786440 | tf_op jit(solution)/shard_map/kv_bwd_far/ppermute | solution.py:35
  22.7 27.3 %collective-permute-start.1 = (bf16[1,128,4096]{2,1,0:T(8,128)(2,1)}, bf16[1,128,4096]{2,1,0:T(8,128)(2,1)S(1)}, u32[]{:S(2)}, u32[]{:S(2)}) collective-permute-start(bf16[1,128,4096]{2,1,0:T(8,128)(2,1)} %param.9), channel_id=1, source_target_pairs={{0,16},{16,32},{32,48},{48,64},{64,80},{80,96},{96,112},{112,128},... | collective-permute-start | bytes 3145736 | tf_op jit(solution)/shard_map/query_moved/ppermute | solution.py:35
  23.5 1.0 %copy-start = (bf16[1,128,1024]{2,1,0:T(8,128)(2,1)S(1)}, bf16[1,128,1024]{2,1,0:T(8,128)(2,1)}, u32[]{:S(2)}) copy-start(bf16[1,128,1024]{2,1,0:T(8,128)(2,1)} %get-tuple-element.21.refs_3_.refs_7_) | copy-start | bytes 786436
  24.4 1.2 %copy-start.1 = (bf16[1,128,4096]{2,1,0:T(8,128)(2,1)S(1)}, bf16[1,128,4096]{2,1,0:T(8,128)(2,1)}, u32[]{:S(2)}) copy-start(bf16[1,128,4096]{2,1,0:T(8,128)(2,1)} %query_ref.3) | copy-start | bytes 3145732
  25.7 0.7 %copy-start.3 = (s32[1,16]{1,0:T(1,128)S(1)}, s32[1,16]{1,0:T(1,128)}, u32[]{:S(2)}) copy-start(s32[1,16]{1,0:T(1,128)} %len_ref.3) | copy-start | bytes 196
  30.5 13.1 %collective-permute-start.6 = (bf16[1,128,1152]{2,1,0:T(8,128)(2,1)S(1)}, bf16[1,128,1152]{2,1,0:T(8,128)(2,1)S(1)}, u32[]{:S(2)}, u32[]{:S(2)}) collective-permute-start(bf16[1,128,1152]{2,1,0:T(8,128)(2,1)S(1)} %collective-permute-done.first_ref.refs_3_.refs_7_), channel_id=1, source_target_pairs={{0,2},{1,3},{2,4},{3,5},{4,6},{5,7},{6,8},{7,9},{8,10},{9,11},{10,... | collective-permute-start | bytes 884744 | tf_op jit(solution)/shard_map/kv_fwd_middle/ppermute | solution.py:35
  40.2 4.0 %collective-permute-start.10 = (bf16[1,128,1024]{2,1,0:T(8,128)(2,1)S(1)}, bf16[1,128,1024]{2,1,0:T(8,128)(2,1)S(1)}, u32[]{:S(2)}, u32[]{:S(2)}) collective-permute-start(bf16[1,128,1024]{2,1,0:T(8,128)(2,1)S(1)} %get-tuple-element.28), channel_id=1, source_target_pairs={{0,15},{1,0},{2,1},{3,2},{4,3},{5,4},{6,5},{7,6},{8,7},{9,8},{10,9... | collective-permute-start | bytes 786440 | tf_op jit(solution)/shard_map/part_far/ppermute | solution.py:35
  40.2 4.0 %collective-permute-start.9 = (bf16[1,128,1024]{2,1,0:T(8,128)(2,1)S(1)}, bf16[1,128,1024]{2,1,0:T(8,128)(2,1)S(1)}, u32[]{:S(2)}, u32[]{:S(2)}) collective-permute-start(bf16[1,128,1024]{2,1,0:T(8,128)(2,1)S(1)} %get-tuple-element.26), channel_id=1, source_target_pairs={{0,1},{1,0},{2,3},{3,2},{4,5},{5,4},{6,7},{7,6},{8,9},{9,8},{10,11... | collective-permute-start | bytes 786440 | tf_op jit(solution)/shard_map/part_near/ppermute | solution.py:41
  43.6 6.4 %collective-permute-start.8 = (bf16[1,128,1152]{2,1,0:T(8,128)(2,1)S(1)}, bf16[1,128,1152]{2,1,0:T(8,128)(2,1)S(1)}, u32[]{:S(2)}, u32[]{:S(2)}) collective-permute-start(bf16[1,128,1152]{2,1,0:T(8,128)(2,1)S(1)} %broadcast_select_fusion), channel_id=1, source_target_pairs={{0,1},{1,0},{2,3},{3,2},{4,5},{5,4},{6,7},{7,6},{8,9},{9,8},{10,11... | collective-permute-start | bytes 884744 | tf_op jit(solution)/shard_map/kv_fwd_near/ppermute | solution.py:41
  43.8 6.2 %collective-permute-start.7 = (bf16[1,128,1152]{2,1,0:T(8,128)(2,1)S(1)}, bf16[1,128,1152]{2,1,0:T(8,128)(2,1)S(1)}, u32[]{:S(2)}, u32[]{:S(2)}) collective-permute-start(bf16[1,128,1152]{2,1,0:T(8,128)(2,1)S(1)} %collective-permute-done.6.refs_1_.refs_5_), channel_id=1, source_target_pairs={{0,1},{1,2},{2,3},{3,4},{4,5},{5,6},{6,7},{7,8},{8,9},{9,10},{10,1... | collective-permute-start | bytes 884744 | tf_op jit(solution)/shard_map/kv_fwd_far/ppermute | solution.py:35
  50.0 7.6 %collective-permute-start.11 = (bf16[1,128,1024]{2,1,0:T(8,128)(2,1)S(1)}, bf16[1,128,1024]{2,1,0:T(8,128)(2,1)S(1)}, u32[]{:S(2)}, u32[]{:S(2)}) collective-permute-start(bf16[1,128,1024]{2,1,0:T(8,128)(2,1)S(1)} %add_convert_fusion), channel_id=1, source_target_pairs={{0,14},{1,15},{2,0},{3,1},{4,2},{5,3},{6,4},{7,5},{8,6},{9,7},{10,... | collective-permute-start | bytes 786440 | tf_op jit(solution)/shard_map/part_fold/ppermute | solution.py:35

commit v4 on v2

--- a/solution.py
+++ b/solution.py
@@ -26,6 +26,7 @@
 VMEM = 24 * 1024 * 1024
 COST = 1
 PACK_COST = 1
+PACK_STEPS = 2
 PACK_VMEM = 56 * 1024 * 1024
 SMALL_VMEM = 8 * 1024 * 1024
 NT = (((1,), (1,)), ((), ()))
@@ -59,10 +60,10 @@
     return pl.CostEstimate(flops=flops, bytes_accessed=bytes_accessed, transcendentals=0)
 
 
-def first_keys(len_ref, columns):
+def first_keys(len_ref, rows=ROWS, offset=0):
     shard = lax.axis_index("ctx")
-    query = shard * ROWS + lax.broadcasted_iota(jnp.int32, (ROWS, columns), 0)
-    start = jnp.zeros((ROWS, columns), jnp.int32)
+    query = shard * ROWS + offset + lax.broadcasted_iota(jnp.int32, (rows, ROWS), 0)
+    start = jnp.zeros((rows, ROWS), jnp.int32)
     end = jnp.int32(0)
     for doc in range(DOCS):
         end = end + len_ref[0, doc]
@@ -121,7 +122,7 @@
 
     @pl.when(pl.program_id(0) == 0)
     def _():
-        fill_bias(first_keys(len_ref, ROWS), bias_ref)
+        fill_bias(first_keys(len_ref), bias_ref)
 
     keys = stacked(key_refs)
     for first in range(0, GROUP, HEADS_AT_ONCE):
@@ -186,9 +187,10 @@
     ):
         out_ref[0, :, :KV_WIDTH] = key_ref[0]
         out_ref[0, :, KV_WIDTH : 2 * KV_WIDTH] = value_ref[0]
-    first = first_keys(len_ref, ROWS)
+    rows = ROWS // PACK_STEPS
+    first = first_keys(len_ref, rows, pl.program_id(0) * rows)
     high = jnp.where(first >= 256, 1, 0)
-    left = lax.broadcasted_iota(jnp.int32, (ROWS, ROWS), 1) < ROWS // 2
+    left = lax.broadcasted_iota(jnp.int32, (rows, ROWS), 1) < ROWS // 2
     coded = jnp.where(left, high, first - 256 * high)
     fwd_ref[0, :, 2 * KV_WIDTH :] = coded.astype(jnp.float32).astype(jnp.bfloat16)
 
@@ -198,10 +200,10 @@
     return small_call(
         pack_kernel,
         (lengths, *keys_and_values),
-        [pl.BlockSpec(memory_space=pltpu.SMEM)] + [row_spec(KV_WIDTH, 1)] * 4,
+        [pl.BlockSpec(memory_space=pltpu.SMEM)] + [row_spec(KV_WIDTH, PACK_STEPS)] * 4,
         [(1, ROWS, width) for width in widths],
-        [row_spec(width, 1) for width in widths],
-        1,
+        [row_spec(width, PACK_STEPS) for width in widths],
+        PACK_STEPS,
         PACK_VMEM,
         PACK_COST,
     )

time: 58.3 us -> 58.2 us (level)
  no operation moved by 1% of the time
where the time goes in v4:
time: 58.2 us; the launch traced here: 58 us
  waiting for transfers between devices  23.9 us (41%)
  Pallas kernels  18.3 us (31%)
  starting transfers between devices  11.1 us (19%)
  local copies, waits for them, and re-layouts  2.83 us (5%)
  other arithmetic  1.14 us (2%)
  between operations  0.71 us (1%)
    ppermute x9, waiting for transfers between devices, from_behind(): lax.ppermute(value, axis, [(at, (at + steps) % count) for at in range(cou...  23.9 us
    ppermute x9, starting transfers between devices, from_behind(): lax.ppermute(value, axis, [(at, (at + steps) % count) for at in range(cou...  10.4 us
    pallas_call x1, Pallas kernels, backward(): pl.pallas_call(backward_kernel, grid=(groups,), out_shape=[jax.ShapeDtype...  6.24 us
    pallas_call x1, Pallas kernels, forward(): pl.pallas_call(forward_kernel, grid=(KV_HEADS,), out_shape=jax.ShapeDtype...  5.16 us
    pallas_call x1, Pallas kernels, probabilities(): pl.pallas_call(probs_kernel, grid=(KV_HEADS,), out_shape=jax.ShapeDtypeSt...  4.15 us
    unnamed x8, local copies, waits for them, and re-layouts  2.83 us
    pallas_call x2, Pallas kernels, small_call(): pl.pallas_call(kernel, grid=(steps,), out_shape=[jax.ShapeDtypeStruct(sha...  2.73 us
  transfers between devices with their start and end apart: 12, of which 6 were waited for; matrix products, arithmetic and copies ran while one was open for 2% of the time, Pallas kernels for 27%

profile of v4, /device:TPU:96, one launch (start us, length us, event | category | flops | bytes accessed | tf_op | source)
XLA Modules:
  0.0 58.0 jit_solution(4129722201575949837)
XLA Ops:
  0.6 0.0 copy-start.1
  0.6 1.9 %shard_map.120 = (bf16[1,128,1152]{2,1,0:T(8,128)(2,1)}, bf16[1,128,1024]{2,1,0:T(8,128)(2,1)}) custom-call(s32[1,16]{1,0:T(1,128)} %len_ref.2, bf16[1,128,512]{2,1,0:T(8,128)(2,1)} %key_fwd.1, bf16[1,128,512]{2,1,0:T(8,128)(2,1)} %value_fwd.1, bf16[1,128,512]{2,1,0:T(8,128)(2,1)} %key_bwd.1, bf16[1,128,512]{2,1,0:T(8,128)(2,1)} %value_bwd.1), custom_call_target="tpu_custom_call" | custom-call | flops 1 | bytes 1 | tf_op jit(solution)/shard_map/pallas_call | solution.py:168
  2.5 3.1 %collective-permute-start.2 = (bf16[1,128,1024]{2,1,0:T(8,128)(2,1)}, bf16[1,128,1024]{2,1,0:T(8,128)(2,1)S(1)}, u32[]{:S(2)}, u32[]{:S(2)}) collective-permute-start(bf16[1,128,1024]{2,1,0:T(8,128)(2,1)} %get-tuple-element.21.refs_3_.refs_7_), channel_id=1, source_target_pairs={{0,2},{1,3},{2,4},{3,5},{4,6},{5,7},{6,8},{7,9},{8,10},{9,11},{10,... | collective-permute-start | bytes 786440 | tf_op jit(solution)/shard_map/kv_bwd_middle/ppermute | solution.py:38
  5.7 5.2 %collective-permute-start.8 = (bf16[1,128,4096]{2,1,0:T(8,128)(2,1)}, bf16[1,128,4096]{2,1,0:T(8,128)(2,1)S(1)}, u32[]{:S(2)}, u32[]{:S(2)}) collective-permute-start(bf16[1,128,4096]{2,1,0:T(8,128)(2,1)} %param.17), channel_id=1, source_target_pairs={{0,240},{16,0},{32,16},{48,32},{64,48},{80,64},{96,80},{112,96},{1... | collective-permute-start | bytes 3145736 | tf_op jit(solution)/shard_map/grad/ppermute | solution.py:38
  10.9 0.0 collective-permute-start
  10.9 0.7 %collective-permute-done.2.refs_1_.refs_5_ = bf16[1,128,1024]{2,1,0:T(8,128)(2,1)S(1)} collective-permute-done((bf16[1,128,1024]{2,1,0:T(8,128)(2,1)}, bf16[1,128,1024]{2,1,0:T(8,128)(2,1)S(1)}, u32[]{:S(2)}, u32[]{:S(2)}) %collective-permute-start.2) | collective-permute-done | bytes 262176 | tf_op jit(solution)/shard_map/kv_bwd_middle/ppermute | solution.py:38
  11.6 1.0 %broadcast_select_fusion.1 = bf16[1,128,1024]{2,1,0:T(8,128)(2,1)S(1)} fusion(bf16[1,128,1024]{2,1,0:T(8,128)(2,1)S(1)} %collective-permute-done.2.refs_1_.refs_5_, bf16[1,128,1024]{2,1,0:T(8,128)(2,1)} %get-tuple-element.21.refs_3_.refs_7_, pred[]{:T(512)S(6)} %eq.2), kind=kLoop, calls=%fused_computation.2 | loop fusion | flops 131072 | bytes 786433 | tf_op jit(solution)/shard_map/jit(_where)/select_n | solution.py:334
  12.5 0.1 collective-permute-start.4
  12.6 0.5 collective-permute-start.3
  13.1 9.5 %collective-permute-done.first_ref.refs_3_.refs_7_ = bf16[1,128,1152]{2,1,0:T(8,128)(2,1)S(1)} collective-permute-done((bf16[1,128,1152]{2,1,0:T(8,128)(2,1)}, bf16[1,128,1152]{2,1,0:T(8,128)(2,1)S(1)}, u32[]{:S(2)}, u32[]{:S(2)}) %collective-permute-start) | collective-permute-done | bytes 294944 | tf_op jit(solution)/shard_map/kv_moved/ppermute | solution.py:38
  22.6 0.0 collective-permute-start.1
  22.6 0.0 collective-permute-done.4.refs_2_.refs_6_
  22.6 0.0 collective-permute-done.3.refs_0_.refs_4_
  22.6 0.0 copy-start
  22.6 1.2 %copy-done = bf16[1,128,4096]{2,1,0:T(8,128)(2,1)S(1)} copy-done((bf16[1,128,4096]{2,1,0:T(8,128)(2,1)S(1)}, bf16[1,128,4096]{2,1,0:T(8,128)(2,1)}, u32[]{:S(2)}) %copy-start) | copy-done | bytes 1048600
  23.8 0.0 copy-start.2
  23.8 0.9 %copy-done.2 = bf16[1,128,1024]{2,1,0:T(8,128)(2,1)S(1)} copy-done((bf16[1,128,1024]{2,1,0:T(8,128)(2,1)S(1)}, bf16[1,128,1024]{2,1,0:T(8,128)(2,1)}, u32[]{:S(2)}) %copy-start.2) | copy-done | bytes 262168
  24.8 0.0 copy-start.3
  24.8 0.7 %copy-done.3 = s32[1,16]{1,0:T(1,128)S(1)} copy-done((s32[1,16]{1,0:T(1,128)S(1)}, s32[1,16]{1,0:T(1,128)}, u32[]{:S(2)}) %copy-start.3) | copy-done | bytes 88
  25.4 4.2 %shard_map.121.probs_ref = f32[4,1024,512]{2,1,0:T(8,128)S(1)} custom-call(s32[1,16]{1,0:T(1,128)S(1)} %copy-done.3, bf16[1,128,4096]{2,1,0:T(8,128)(2,1)S(1)} %copy-done, bf16[1,128,1024]{2,1,0:T(8,128)(2,1)S(1)} %collective-permute-done.3.refs_0_.refs_4_, bf16[1,128,1024]{2,1,0:T(8,128)(2,1)S(1)} %collective-permute-done.2.refs_1_.refs_5_, ...), custom_call_target="tpu_custom_call" | custom-call | flops 1 | bytes 1 | tf_op jit(solution)/shard_map/pallas_call | solution.py:253
  29.6 1.1 %collective-permute-start.5 = (bf16[1,128,1152]{2,1,0:T(8,128)(2,1)S(1)}, bf16[1,128,1152]{2,1,0:T(8,128)(2,1)S(1)}, u32[]{:S(2)}, u32[]{:S(2)}) collective-permute-start(bf16[1,128,1152]{2,1,0:T(8,128)(2,1)S(1)} %collective-permute-done.first_ref.refs_3_.refs_7_), channel_id=1, source_target_pairs={{0,2},{1,3},{2,4},{3,5},{4,6},{5,7},{6,8},{7,9},{8,10},{9,11},{10,... | collective-permute-start | bytes 884744 | tf_op jit(solution)/shard_map/kv_fwd_middle/ppermute | solution.py:38
  30.7 2.6 %collective-permute-done.8.grad_ref = bf16[1,128,4096]{2,1,0:T(8,128)(2,1)S(1)} collective-permute-done((bf16[1,128,4096]{2,1,0:T(8,128)(2,1)}, bf16[1,128,4096]{2,1,0:T(8,128)(2,1)S(1)}, u32[]{:S(2)}, u32[]{:S(2)}) %collective-permute-start.8) | collective-permute-done | bytes 1048608 | tf_op jit(solution)/shard_map/grad/ppermute | solution.py:38
  33.3 0.0 copy-done.1
  33.3 6.2 %shard_map.123 = (bf16[1,128,4096]{2,1,0:T(8,128)(2,1)}, bf16[1,128,1024]{2,1,0:T(8,128)(2,1)S(1)}, bf16[1,128,1024]{2,1,0:T(8,128)(2,1)S(1)}, bf16[1,128,1024]{...) custom-call(f32[4,1024,512]{2,1,0:T(8,128)S(1)} %shard_map.121.probs_ref, bf16[1,128,4096]{2,1,0:T(8,128)(2,1)S(1)} %copy-done.1, ...), custom_call_target="tpu_custom_call" | custom-call | flops 1 | bytes 1 | tf_op jit(solution)/shard_map/pallas_call | solution.py:275
  39.6 0.0 collective-permute-start.10
  39.6 0.5 collective-permute-start.9
  40.1 0.0 collective-permute-done.5.refs_1_.refs_5_
  40.1 0.1 collective-permute-start.7
  40.2 0.5 collective-permute-start.6
  40.7 2.7 %collective-permute-done.10 = bf16[1,128,1024]{2,1,0:T(8,128)(2,1)S(1)} collective-permute-done((bf16[1,128,1024]{2,1,0:T(8,128)(2,1)S(1)}, bf16[1,128,1024]{2,1,0:T(8,128)(2,1)S(1)}, u32[]{:S(2)}, u32[]{:S(2)}) %collective-permute-start.10) | collective-permute-done | bytes 262176 | tf_op jit(solution)/shard_map/part_far_0/ppermute | solution.py:38
  43.5 0.0 collective-permute-done.9.refs_1_
  43.5 0.1 add_convert_fusion
  43.6 5.9 %collective-permute-done.1.query_ref = bf16[1,128,4096]{2,1,0:T(8,128)(2,1)S(1)} collective-permute-done((bf16[1,128,4096]{2,1,0:T(8,128)(2,1)}, bf16[1,128,4096]{2,1,0:T(8,128)(2,1)S(1)}, u32[]{:S(2)}, u32[]{:S(2)}) %collective-permute-start.1) | collective-permute-done | bytes 1048608 | tf_op jit(solution)/shard_map/query_moved/ppermute | solution.py:38
  49.5 0.0 collective-permute-start.11
  49.5 0.0 collective-permute-done.7.refs_2_.refs_6_
  49.6 0.0 collective-permute-done.6.refs_0_.refs_4_
  49.6 5.2 %shard_map.122 = bf16[1,128,4096]{2,1,0:T(8,128)(2,1)} custom-call(bf16[1,128,1152]{2,1,0:T(8,128)(2,1)S(1)} %collective-permute-done.first_ref.refs_3_.refs_7_, bf16[1,128,4096]{2,1,0:T(8,128)(2,1)S(1)} %collective-permute-done.1.query_ref, bf16[1,128,1152]{2,1,0:T(8,128)(2,1)S(1)} %collective-permute-done.6.refs_0_.refs_4_, ...), custom_call_target="tpu_custom_call" | custom-call | flops 1 | bytes 1 | tf_op jit(solution)/shard_map/pallas_call | solution.py:234
  54.7 2.4 %collective-permute-done.11.refs_2_ = bf16[1,128,1024]{2,1,0:T(8,128)(2,1)S(1)} collective-permute-done((bf16[1,128,1024]{2,1,0:T(8,128)(2,1)S(1)}, bf16[1,128,1024]{2,1,0:T(8,128)(2,1)S(1)}, u32[]{:S(2)}, u32[]{:S(2)}) %collective-permute-start.11) | collective-permute-done | bytes 262176 | tf_op jit(solution)/shard_map/part_fold_0/ppermute | solution.py:38
  57.1 0.8 %shard_map.124 = (bf16[1,128,512]{2,1,0:T(8,128)(2,1)}, bf16[1,128,512]{2,1,0:T(8,128)(2,1)}) custom-call(bf16[1,128,1024]{2,1,0:T(8,128)(2,1)S(1)} %get-tuple-element.25.refs_0_, bf16[1,128,1024]{2,1,0:T(8,128)(2,1)S(1)} %collective-permute-done.9.refs_1_, bf16[1,128,1024]{2,1,0:T(8,128)(2,1)S(1)} %collective-permute-done.11.refs_2_), custom_call_target="tpu_custom_call" | custom-call | flops 1 | bytes 1 | tf_op jit(solution)/shard_map/pallas_call | solution.py:168
  (1 shorter events, 0.0 us)
Async XLA Ops:
  0.6 32.7 %copy-start.1 = (bf16[1,128,4096]{2,1,0:T(8,128)(2,1)S(1)}, bf16[1,128,4096]{2,1,0:T(8,128)(2,1)}, u32[]{:S(2)}) copy-start(bf16[1,128,4096]{2,1,0:T(8,128)(2,1)} %query_ref.3) | copy-start | bytes 3145732
  2.5 9.0 %collective-permute-start.2 = (bf16[1,128,1024]{2,1,0:T(8,128)(2,1)}, bf16[1,128,1024]{2,1,0:T(8,128)(2,1)S(1)}, u32[]{:S(2)}, u32[]{:S(2)}) collective-permute-start(bf16[1,128,1024]{2,1,0:T(8,128)(2,1)} %get-tuple-element.21.refs_3_.refs_7_), channel_id=1, source_target_pairs={{0,2},{1,3},{2,4},{3,5},{4,6},{5,7},{6,8},{7,9},{8,10},{9,11},{10,... | collective-permute-start | bytes 786440 | tf_op jit(solution)/shard_map/kv_bwd_middle/ppermute | solution.py:38
  5.7 27.7 %collective-permute-start.8 = (bf16[1,128,4096]{2,1,0:T(8,128)(2,1)}, bf16[1,128,4096]{2,1,0:T(8,128)(2,1)S(1)}, u32[]{:S(2)}, u32[]{:S(2)}) collective-permute-start(bf16[1,128,4096]{2,1,0:T(8,128)(2,1)} %param.17), channel_id=1, source_target_pairs={{0,240},{16,0},{32,16},{48,32},{64,48},{80,64},{96,80},{112,96},{1... | collective-permute-start | bytes 3145736 | tf_op jit(solution)/shard_map/grad/ppermute | solution.py:38
  10.9 11.7 %collective-permute-start = (bf16[1,128,1152]{2,1,0:T(8,128)(2,1)}, bf16[1,128,1152]{2,1,0:T(8,128)(2,1)S(1)}, u32[]{:S(2)}, u32[]{:S(2)}) collective-permute-start(bf16[1,128,1152]{2,1,0:T(8,128)(2,1)} %get-tuple-element.18), channel_id=1, source_target_pairs={{0,16},{16,32},{32,48},{48,64},{64,80},{80,96},{96,112},{112,128},... | collective-permute-start | bytes 884744 | tf_op jit(solution)/shard_map/kv_moved/ppermute | solution.py:38
  12.5 10.1 %collective-permute-start.4 = (bf16[1,128,1024]{2,1,0:T(8,128)(2,1)S(1)}, bf16[1,128,1024]{2,1,0:T(8,128)(2,1)S(1)}, u32[]{:S(2)}, u32[]{:S(2)}) collective-permute-start(bf16[1,128,1024]{2,1,0:T(8,128)(2,1)S(1)} %broadcast_select_fusion.1), channel_id=1, source_target_pairs={{0,1},{1,0},{2,3},{3,2},{4,5},{5,4},{6,7},{7,6},{8,9},{9,8},{10,11... | collective-permute-start | bytes 786440 | tf_op jit(solution)/shard_map/kv_bwd_near/ppermute | solution.py:44
  12.6 10.0 %collective-permute-start.3 = (bf16[1,128,1024]{2,1,0:T(8,128)(2,1)S(1)}, bf16[1,128,1024]{2,1,0:T(8,128)(2,1)S(1)}, u32[]{:S(2)}, u32[]{:S(2)}) collective-permute-start(bf16[1,128,1024]{2,1,0:T(8,128)(2,1)S(1)} %collective-permute-done.2.refs_1_.refs_5_), channel_id=1, source_target_pairs={{0,1},{1,2},{2,3},{3,4},{4,5},{5,6},{6,7},{7,8},{8,9},{9,10},{10,1... | collective-permute-start | bytes 786440 | tf_op jit(solution)/shard_map/kv_bwd_far/ppermute | solution.py:38
  22.6 26.9 %collective-permute-start.1 = (bf16[1,128,4096]{2,1,0:T(8,128)(2,1)}, bf16[1,128,4096]{2,1,0:T(8,128)(2,1)S(1)}, u32[]{:S(2)}, u32[]{:S(2)}) collective-permute-start(bf16[1,128,4096]{2,1,0:T(8,128)(2,1)} %param.9), channel_id=1, source_target_pairs={{0,16},{16,32},{32,48},{48,64},{64,80},{80,96},{96,112},{112,128},... | collective-permute-start | bytes 3145736 | tf_op jit(solution)/shard_map/query_moved/ppermute | solution.py:38
  22.6 1.2 %copy-start = (bf16[1,128,4096]{2,1,0:T(8,128)(2,1)S(1)}, bf16[1,128,4096]{2,1,0:T(8,128)(2,1)}, u32[]{:S(2)}) copy-start(bf16[1,128,4096]{2,1,0:T(8,128)(2,1)} %query_ref.3) | copy-start | bytes 3145732
  23.8 0.9 %copy-start.2 = (bf16[1,128,1024]{2,1,0:T(8,128)(2,1)S(1)}, bf16[1,128,1024]{2,1,0:T(8,128)(2,1)}, u32[]{:S(2)}) copy-start(bf16[1,128,1024]{2,1,0:T(8,128)(2,1)} %get-tuple-element.21.refs_3_.refs_7_) | copy-start | bytes 786436
  24.8 0.7 %copy-start.3 = (s32[1,16]{1,0:T(1,128)S(1)}, s32[1,16]{1,0:T(1,128)}, u32[]{:S(2)}) copy-start(s32[1,16]{1,0:T(1,128)} %len_ref.3) | copy-start | bytes 196
  29.6 10.5 %collective-permute-start.5 = (bf16[1,128,1152]{2,1,0:T(8,128)(2,1)S(1)}, bf16[1,128,1152]{2,1,0:T(8,128)(2,1)S(1)}, u32[]{:S(2)}, u32[]{:S(2)}) collective-permute-start(bf16[1,128,1152]{2,1,0:T(8,128)(2,1)S(1)} %collective-permute-done.first_ref.refs_3_.refs_7_), channel_id=1, source_target_pairs={{0,2},{1,3},{2,4},{3,5},{4,6},{5,7},{6,8},{7,9},{8,10},{9,11},{10,... | collective-permute-start | bytes 884744 | tf_op jit(solution)/shard_map/kv_fwd_middle/ppermute | solution.py:38
  39.6 3.9 %collective-permute-start.10 = (bf16[1,128,1024]{2,1,0:T(8,128)(2,1)S(1)}, bf16[1,128,1024]{2,1,0:T(8,128)(2,1)S(1)}, u32[]{:S(2)}, u32[]{:S(2)}) collective-permute-start(bf16[1,128,1024]{2,1,0:T(8,128)(2,1)S(1)} %get-tuple-element.28), channel_id=1, source_target_pairs={{0,15},{1,0},{2,1},{3,2},{4,3},{5,4},{6,5},{7,6},{8,7},{9,8},{10,9... | collective-permute-start | bytes 786440 | tf_op jit(solution)/shard_map/part_far_0/ppermute | solution.py:38
  39.6 3.9 %collective-permute-start.9 = (bf16[1,128,1024]{2,1,0:T(8,128)(2,1)S(1)}, bf16[1,128,1024]{2,1,0:T(8,128)(2,1)S(1)}, u32[]{:S(2)}, u32[]{:S(2)}) collective-permute-start(bf16[1,128,1024]{2,1,0:T(8,128)(2,1)S(1)} %get-tuple-element.26), channel_id=1, source_target_pairs={{0,1},{1,0},{2,3},{3,2},{4,5},{5,4},{6,7},{7,6},{8,9},{9,8},{10,11... | collective-permute-start | bytes 786440 | tf_op jit(solution)/shard_map/part_near_0/ppermute | solution.py:44
  40.1 9.4 %collective-permute-start.7 = (bf16[1,128,1152]{2,1,0:T(8,128)(2,1)S(1)}, bf16[1,128,1152]{2,1,0:T(8,128)(2,1)S(1)}, u32[]{:S(2)}, u32[]{:S(2)}) collective-permute-start(bf16[1,128,1152]{2,1,0:T(8,128)(2,1)S(1)} %broadcast_select_fusion), channel_id=1, source_target_pairs={{0,1},{1,0},{2,3},{3,2},{4,5},{5,4},{6,7},{7,6},{8,9},{9,8},{10,11... | collective-permute-start | bytes 884744 | tf_op jit(solution)/shard_map/kv_fwd_near/ppermute | solution.py:44
  40.2 9.3 %collective-permute-start.6 = (bf16[1,128,1152]{2,1,0:T(8,128)(2,1)S(1)}, bf16[1,128,1152]{2,1,0:T(8,128)(2,1)S(1)}, u32[]{:S(2)}, u32[]{:S(2)}) collective-permute-start(bf16[1,128,1152]{2,1,0:T(8,128)(2,1)S(1)} %collective-permute-done.5.refs_1_.refs_5_), channel_id=1, source_target_pairs={{0,1},{1,2},{2,3},{3,4},{4,5},{5,6},{6,7},{7,8},{8,9},{9,10},{10,1... | collective-permute-start | bytes 884744 | tf_op jit(solution)/shard_map/kv_fwd_far/ppermute | solution.py:38
  49.5 7.6 %collective-permute-start.11 = (bf16[1,128,1024]{2,1,0:T(8,128)(2,1)S(1)}, bf16[1,128,1024]{2,1,0:T(8,128)(2,1)S(1)}, u32[]{:S(2)}, u32[]{:S(2)}) collective-permute-start(bf16[1,128,1024]{2,1,0:T(8,128)(2,1)S(1)} %add_convert_fusion), channel_id=1, source_target_pairs={{0,14},{1,15},{2,0},{3,1},{4,2},{5,3},{6,4},{7,5},{8,6},{9,7},{10,... | collective-permute-start | bytes 786440 | tf_op jit(solution)/shard_map/part_fold_0/ppermute | solution.py:38
